TPU v7x, 128 devices: a whole 4x4x4 slice. The times are simulated.
128 devices in a mesh: wide: 16 (over x, y), narrow: 8 (over z, core).
Axes of the slice: x: 4, y: 4, z: 4, core: 2. Of those that a mesh axis runs over, the one named last changes fastest.
Arguments:
- source: float32 [125, 131072], P(None, ('wide', 'narrow')), may hold values from -6 to 6
- inverses: float32 [4, 125, 125], replicated, may hold values from -0.3 to 2.3, as said below
- lift: float32 [125, 150], replicated, may hold values from -0.5 to 0.5
- stab: float32 [4], replicated, may hold values from 1 to 4
- material: int32 [131072], P(('wide', 'narrow')), may hold values from 0 to 3
- face_slot: int32 [6, 131072], P(None, ('wide', 'narrow')), may hold values from 0 to 3839, as said below
- owner_map: int32 [128, 768], P(('wide', 'narrow')), may hold values from 0 to 3072, as said below
Outputs:
- potential: float32 [125, 131072], P(None, ('wide', 'narrow'))
- trace_own: float32 [25, 393216], P(None, ('wide', 'narrow'))
Inputs may be any that keep to these rules, and one draw needn't show every extreme that they name: `face_slot`: values below 3072 are faces the device owns, each named by some element of the device; 3072 + g is ghost slot g, named at most once and only where the neighbour's owner_map names it; a device holds at most 256 faces from a neighbour along the gap length and 128 across, both reached. `owner_map`: entry j of segment k of device d is the owned face that the neighbour of segment k holds in slot j of the opposite segment, or 3072 where it holds none; the faces named on one device are distinct. `inverses`: symmetric with a positive diagonal.
All inputs are finite; a program needn't handle non-finite values.
Results may differ from a plain program's by a relative error of at most 0.0001.
Values sent between devices are 32-bit elements; how exact they have to be, the bound alone decides.
A program may use at most 64 MiB of HBM per device.

v0:
```python
import math

import jax
import jax.numpy as jnp
from jax import lax
from jax.sharding import PartitionSpec as P

SWEEPS = 3


HIGH = lax.Precision.HIGHEST
damping = 0.6


def with_halo(cells, sides, width):
    for axis, dim in sides:
        count = lax.axis_size(axis)
        ends = count - 1
        head = lax.slice_in_dim(cells, 0, width, axis=dim)
        tail = lax.slice_in_dim(cells, cells.shape[dim] - width, cells.shape[dim], axis=dim)
        cells = jnp.concatenate(
            [
                lax.ppermute(tail, axis, [(i, (i + 1) % count) for i in range(ends)]),
                cells,
                lax.ppermute(head, axis, [((i + 1) % count, i) for i in range(ends)]),
            ],
            axis=dim,
        )
    return cells


def per_material(inverses, material, values):
    result = jnp.zeros(values.shape, jnp.float32)
    for mat_id in range(inverses.shape[0]):
        product = jnp.dot(
            inverses[mat_id], values, precision=HIGH, preferred_element_type=jnp.float32
        )
        result = result + jnp.where(material[None, :] == mat_id, product, jnp.float32(0.0))
    return result


def per_element(table_rows, material):
    result = jnp.zeros((table_rows.shape[1], material.shape[0]), jnp.float32)
    for mat_id in range(table_rows.shape[0]):
        result = result + jnp.where(
            material[None, :] == mat_id, table_rows[mat_id][:, None], jnp.float32(0.0)
        )
    return result


def trace_diagonal(inverses, lift, stab):
    applied = jnp.einsum("mij,jt->mit", inverses, lift, precision=HIGH)
    return stab[:, None] + jnp.abs(jnp.sum(lift[None, :, :] * applied, axis=1))


def element_terms(values, lift, inverses, material, stab_cols):
    lifted = jnp.dot(lift, values, precision=HIGH, preferred_element_type=jnp.float32)
    solved = per_material(inverses, material, lifted)
    return stab_cols * values + jnp.dot(
        lift.T, solved, precision=HIGH, preferred_element_type=jnp.float32
    )


def side_blocks(face_slot):
    slots = face_slot.reshape(-1)
    block_size = math.gcd(slots.shape[0], 512)
    return (slots.reshape(slots.shape[0] // block_size, block_size), block_size)


def assemble(terms, face_slot, table_width):
    slot_blocks, block_size = side_blocks(face_slot)
    block_count = slot_blocks.shape[0]
    row_count = terms.shape[0] // 6
    term_blocks = terms.reshape(row_count, block_count, block_size).transpose(1, 0, 2)
    columns = jnp.arange(table_width, dtype=jnp.int32)

    def add_block(running, block_pair):
        term_block, slot_block = block_pair
        selector = (slot_block[:, None] == columns[None, :]).astype(jnp.float32)
        return (
            running
            + jnp.dot(term_block, selector, precision=HIGH, preferred_element_type=jnp.float32),
            None,
        )

    result, unused = lax.scan(
        add_block, jnp.zeros((row_count, table_width), jnp.float32), (term_blocks, slot_blocks)
    )
    return result


def element_values(trace_table, face_slot, fnodes):
    slot_blocks, block_size = side_blocks(face_slot)
    block_count = slot_blocks.shape[0]
    columns = jnp.arange(trace_table.shape[1], dtype=jnp.int32)

    def take_block(carried, slot_block):
        selector = (columns[:, None] == slot_block[None, :]).astype(jnp.float32)
        return (
            carried,
            jnp.dot(trace_table, selector, precision=HIGH, preferred_element_type=jnp.float32),
        )

    unused, picked = lax.scan(take_block, jnp.float32(0.0), slot_blocks)
    flat_values = picked.transpose(1, 0, 2).reshape(fnodes, block_count * block_size)
    return flat_values.reshape(fnodes * 6, face_slot.shape[1])


def outgoing(table_own, owner_list):
    columns = jnp.arange(table_own.shape[1], dtype=jnp.int32)
    selector = (columns[:, None] == owner_list[None, :]).astype(jnp.float32)
    return jnp.dot(table_own, selector, precision=HIGH, preferred_element_type=jnp.float32)


def add_arrivals(table_own, arrived, owner_list):
    columns = jnp.arange(table_own.shape[1], dtype=jnp.int32)
    selector = (owner_list[:, None] == columns[None, :]).astype(jnp.float32)
    return table_own + jnp.dot(
        arrived, selector, precision=HIGH, preferred_element_type=jnp.float32
    )


def trade_buffers(buffers, cap_wide, cap_narrow):
    wide_part = jnp.stack([buffers[:, :cap_wide], buffers[:, cap_wide : 2 * cap_wide]])
    narrow_part = jnp.stack(
        [
            buffers[:, 2 * cap_wide : 2 * cap_wide + cap_narrow],
            buffers[:, 2 * cap_wide + cap_narrow :],
        ]
    )
    wide_padded = with_halo(wide_part, (("wide", 0),), 1)
    narrow_padded = with_halo(narrow_part, (("narrow", 0),), 1)
    return jnp.concatenate(
        [wide_padded[0], wide_padded[3], narrow_padded[0], narrow_padded[3]], axis=1
    )


def shards(source, inverses, lift, stab, material, face_slot, owner_map):
    elem_count = source.shape[1]
    owned_count = 3 * elem_count
    cap_wide = elem_count // 4
    cap_narrow = elem_count // 8
    fnodes = lift.shape[1] // 6
    owner_list = owner_map.reshape(-1)
    ghosts = owner_list.shape[0]
    table_width = owned_count + ghosts
    base_state = per_material(inverses, material, source)
    stab_cols = per_element(stab[:, None], material)
    rhs_terms = jnp.dot(lift.T, base_state, precision=HIGH, preferred_element_type=jnp.float32)
    diag_terms = per_element(trace_diagonal(inverses, lift, stab), material)
    both_tables = assemble(jnp.concatenate([rhs_terms, diag_terms], axis=0), face_slot, table_width)
    rhs_table = both_tables[:fnodes]
    diag_table = both_tables[fnodes:]
    arrived = trade_buffers(
        jnp.concatenate([rhs_table[:, owned_count:], diag_table[:, owned_count:]], axis=0),
        cap_wide,
        cap_narrow,
    )
    rhs_own = add_arrivals(rhs_table[:, :owned_count], arrived[:fnodes], owner_list)
    diag_own = add_arrivals(diag_table[:, :owned_count], arrived[fnodes:], owner_list)
    trace_own = damping * rhs_own / diag_own
    for sweep_index in range(SWEEPS - 1):
        ghost_values = trade_buffers(outgoing(trace_own, owner_list), cap_wide, cap_narrow)
        trace_table = jnp.concatenate([trace_own, ghost_values], axis=1)
        terms = element_terms(
            element_values(trace_table, face_slot, fnodes), lift, inverses, material, stab_cols
        )
        applied_table = assemble(terms, face_slot, table_width)
        returned = trade_buffers(applied_table[:, owned_count:], cap_wide, cap_narrow)
        applied = add_arrivals(applied_table[:, :owned_count], returned, owner_list)
        trace_own = trace_own + damping * (rhs_own - applied) / diag_own
    ghost_values = trade_buffers(outgoing(trace_own, owner_list), cap_wide, cap_narrow)
    trace_table = jnp.concatenate([trace_own, ghost_values], axis=1)
    lifted = jnp.dot(
        lift,
        element_values(trace_table, face_slot, fnodes),
        precision=HIGH,
        preferred_element_type=jnp.float32,
    )
    potential = base_state - per_material(inverses, material, lifted)
    return (potential, trace_own)


def solution(mesh):
    return jax.shard_map(
        shards,
        mesh=mesh,
        in_specs=(
            P(None, ("wide", "narrow")),
            P(),
            P(),
            P(),
            P(("wide", "narrow")),
            P(None, ("wide", "narrow")),
            P(("wide", "narrow"), None),
        ),
        out_specs=(P(None, ("wide", "narrow")), P(None, ("wide", "narrow"))),
        check_vma=False,
    )
```

profile of v0, /device:TPU:7, one launch (start us, length us, event | category | flops | bytes accessed | tf_op | source)
XLA Modules:
  0.0 377.8 jit_solution(18049990424339644227)
XLA Ops:
  4.7 3.2 select_add_fusion.1
  13.7 54.8 %while.69 = (s32[]{:T(128)}, f32[50,3840]{1,0:T(8,128)S(1)}, f32[12,50,512]{2,0,1:T(8,128)}, s32[12,512]{1,0:T(8,128)S(1)}, s32[]{:T(128)}, /*index=5*/s32[]{:T(128)}) while((s32[]{:T(128)}, f32[50,3840]{1,0:T(8,128)S(1)}, f32[12,50,512]{2,0,1:T(8,128)}, s32[12,512]{1,0:T(8,128)S(1)}, s32[]{:T(128)}, /*index=5*/s32[]{:T(128)}) %tuple.154), condition=%wide.region_2.3_spmd.clone, body=%wide.region_1.2_spmd.clone.sunk | while | flops 1181998080 | bytes 1849431 | solution.py:86
  15.0 3.3 fusion.149
  19.6 3.3 fusion.149
  24.1 3.3 fusion.149
  28.7 3.3 fusion.149
  33.2 3.3 fusion.149
  37.8 3.3 fusion.149
  42.4 3.3 fusion.149
  46.9 3.3 fusion.149
  51.5 3.3 fusion.149
  56.1 3.3 fusion.149
  60.6 3.3 fusion.149
  65.2 3.3 fusion.149
  68.5 3.2 collective-permute-start
  71.7 4.2 %collective-permute-start.1 = (f32[1,50,256]{2,1,0:T(8,128)S(1)}, f32[1,50,256]{2,1,0:T(8,128)S(1)}, u32[]{:S(2)}, u32[]{:S(2)}) collective-permute-start(f32[1,50,256]{2,1,0:T(8,128)S(1)} %get-tuple-element.317), channel_id=1, source_target_pairs={{8,0},{16,8},{24,16},{32,24},{40,32},{48,40},{56,48},{64,56},{72,6... | collective-permute-start | bytes 153608 | tf_op jit(solution)/shard_map/ppermute | solution.py:25
  75.9 4.7 %collective-permute-start.2 = (f32[1,50,128]{2,1,0:T(8,128)S(1)}, f32[1,50,128]{2,1,0:T(8,128)S(1)}, u32[]{:S(2)}, u32[]{:S(2)}) collective-permute-start(f32[1,50,128]{2,1,0:T(8,128)S(1)} %get-tuple-element.318), channel_id=1, source_target_pairs={{0,1},{1,2},{2,3},{3,4},{4,5},{5,6},{6,7},{8,9},{9,10},{10,11},{11... | collective-permute-start | bytes 76808 | tf_op jit(solution)/shard_map/ppermute | solution.py:23
  82.8 3.0 collective-permute-done.3
  85.8 3.5 fusion.47
  89.4 3.6 constant_dynamic-update-slice_fusion.4
  93.0 3.5 fusion.35
  98.4 5.5 %collective-permute-start.5 = (f32[1,25,256]{2,1,0:T(8,128)S(1)}, f32[1,25,256]{2,1,0:T(8,128)S(1)}, u32[]{:S(2)}, u32[]{:S(2)}) collective-permute-start(f32[1,25,256]{2,1,0:T(8,128)S(1)} %get-tuple-element.338), channel_id=1, source_target_pairs={{8,0},{16,8},{24,16},{32,24},{40,32},{48,40},{56,48},{64,56},{72,6... | collective-permute-start | bytes 76808 | tf_op jit(solution)/shard_map/ppermute | solution.py:25
  108.6 2.8 collective-permute-done.7
  111.5 32.9 %while.66 = (s32[]{:T(128)}, f32[12,25,512]{2,1,0:T(8,128)S(1)}, s32[12,512]{1,0:T(8,128)S(1)}, f32[25,3840]{1,0:T(8,128)S(1)}, s32[]{:T(128)}) while((s32[]{:T(128)}, f32[12,25,512]{2,1,0:T(8,128)S(1)}, s32[12,512]{1,0:T(8,128)S(1)}, f32[25,3840]{1,0:T(8,128)S(1)}, s32[]{:T(128)}) %tuple.157), condition=%wide.region_4.5_spmd.clone, body=%wide.region_3.4_spmd.clone.sunk | while | flops 591790080 | bytes 563269 | solution.py:104
  141.7 2.7 fusion.144
  150.3 36.5 %while.70 = (s32[]{:T(128)}, f32[25,3840]{1,0:T(8,128)S(1)}, f32[12,25,512]{2,0,1:T(8,128)S(1)}, s32[12,512]{1,0:T(8,128)S(1)}, s32[]{:T(128)}, /*index=5*/s32[]{:T(128)}) while((s32[]{:T(128)}, f32[25,3840]{1,0:T(8,128)S(1)}, f32[12,25,512]{2,0,1:T(8,128)S(1)}, s32[12,512]{1,0:T(8,128)S(1)}, s32[]{:T(128)}, ...), condition=%wide.region_6.7_spmd.clone, body=%wide.region_5.6_spmd.clone.sunk | while | flops 591982080 | bytes 927831 | solution.py:86
  150.4 2.9 fusion.150
  153.4 2.9 fusion.150
  156.4 2.9 fusion.150
  159.5 2.9 fusion.150
  162.5 2.9 fusion.150
  165.6 2.9 fusion.150
  168.6 2.9 fusion.150
  171.6 2.9 fusion.150
  174.7 2.9 fusion.150
  177.7 2.9 fusion.150
  180.8 2.9 fusion.150
  183.8 2.9 fusion.150
  188.7 5.5 %collective-permute-start.9 = (f32[1,25,256]{2,1,0:T(8,128)S(1)}, f32[1,25,256]{2,1,0:T(8,128)S(1)}, u32[]{:S(2)}, u32[]{:S(2)}) collective-permute-start(f32[1,25,256]{2,1,0:T(8,128)S(1)} %get-tuple-element.325), channel_id=1, source_target_pairs={{8,0},{16,8},{24,16},{32,24},{40,32},{48,40},{56,48},{64,56},{72,6... | collective-permute-start | bytes 76808 | tf_op jit(solution)/shard_map/ppermute | solution.py:25
  201.8 4.6 %constant_dynamic-update-slice_fusion.9 = (f32[25,3840]{1,0:T(8,128)S(1)}, f32[25,3072]{1,0:T(8,128)S(1)}) fusion(f32[25,3072]{1,0:T(8,128)} %copy-done.8, f32[25,3072]{1,0:T(8,128)} %copy-done.6, s32[768]{0:T(1024)S(1)} %reduce, f32[25,128]{1,0:T(8,128)S(1)} %bitcast.261, f32[25,128]{1,0:T(8,128)S(1)} %bitcast.259, f32[25,256]{1,0:T(8,128)S(1)} %bitcast.257, ...), kind=kOutput, calls=%fused_computation.152 | convolution fusion | flops 710743296 | bytes 1787904 | tf_op jit(solution)/shard_map/dot_general | solution.py:118
  206.4 3.4 fusion.34
  211.8 5.5 %collective-permute-start.13 = (f32[1,25,256]{2,1,0:T(8,128)S(1)}, f32[1,25,256]{2,1,0:T(8,128)S(1)}, u32[]{:S(2)}, u32[]{:S(2)}) collective-permute-start(f32[1,25,256]{2,1,0:T(8,128)S(1)} %get-tuple-element.334), channel_id=1, source_target_pairs={{8,0},{16,8},{24,16},{32,24},{40,32},{48,40},{56,48},{64,56},{72,6... | collective-permute-start | bytes 76808 | tf_op jit(solution)/shard_map/ppermute | solution.py:25
  222.0 2.9 collective-permute-done.15
  225.0 32.9 %while.67 = (s32[]{:T(128)}, f32[12,25,512]{2,1,0:T(8,128)S(1)}, s32[12,512]{1,0:T(8,128)S(1)}, f32[25,3840]{1,0:T(8,128)S(1)}, s32[]{:T(128)}) while((s32[]{:T(128)}, f32[12,25,512]{2,1,0:T(8,128)S(1)}, s32[12,512]{1,0:T(8,128)S(1)}, f32[25,3840]{1,0:T(8,128)S(1)}, s32[]{:T(128)}) %tuple.159), condition=%wide.region_8.9_spmd.clone, body=%wide.region_7.8_spmd.clone.sunk | while | flops 591790080 | bytes 563269 | solution.py:104
  263.9 36.5 %while.71 = (s32[]{:T(128)}, f32[25,3840]{1,0:T(8,128)S(1)}, f32[12,25,512]{2,0,1:T(8,128)S(1)}, s32[12,512]{1,0:T(8,128)S(1)}, s32[]{:T(128)}, /*index=5*/s32[]{:T(128)}) while((s32[]{:T(128)}, f32[25,3840]{1,0:T(8,128)S(1)}, f32[12,25,512]{2,0,1:T(8,128)S(1)}, s32[12,512]{1,0:T(8,128)S(1)}, s32[]{:T(128)}, ...), condition=%wide.region_10.11_spmd.clone, body=%wide.region_9.10_spmd.clone.sunk | while | flops 591982080 | bytes 927831 | solution.py:86
  264.0 2.9 fusion.151
  267.0 2.9 fusion.151
  270.1 2.9 fusion.151
  273.1 2.9 fusion.151
  276.2 2.9 fusion.151
  279.2 2.9 fusion.151
  282.2 2.9 fusion.151
  285.3 2.9 fusion.151
  288.3 2.9 fusion.151
  291.4 2.9 fusion.151
  294.4 2.9 fusion.151
  297.5 2.9 fusion.151
  302.4 5.5 %collective-permute-start.17 = (f32[1,25,256]{2,1,0:T(8,128)S(1)}, f32[1,25,256]{2,1,0:T(8,128)S(1)}, u32[]{:S(2)}, u32[]{:S(2)}) collective-permute-start(f32[1,25,256]{2,1,0:T(8,128)S(1)} %get-tuple-element.321), channel_id=1, source_target_pairs={{8,0},{16,8},{24,16},{32,24},{40,32},{48,40},{56,48},{64,56},{72,6... | collective-permute-start | bytes 76808 | tf_op jit(solution)/shard_map/ppermute | solution.py:25
  312.5 2.9 collective-permute-done.19
  315.4 4.8 %constant_dynamic-update-slice_fusion.14 = (f32[25,3840]{1,0:T(8,128)S(1)}, f32[25,3072]{1,0:T(8,128)S(1)}) fusion(f32[25,3072]{1,0:T(8,128)} %copy-done.7, f32[25,3072]{1,0:T(8,128)} %copy-done.8, f32[25,3072]{1,0:T(8,128)} %copy-done.6, s32[768]{0:T(1024)S(1)} %reduce, f32[25,128]{1,0:T(8,128)S(1)} %bitcast.262, f32[25,128]{1,0:T(8,128)S(1)} %bitcast.260, ...), kind=kOutput, calls=%fused_computation.157 | convolution fusion | flops 710589696 | bytes 2095104 | tf_op jit(solution)/shard_map/dot_general | solution.py:118
  320.2 3.4 fusion.33
  325.6 5.5 %collective-permute-start.21 = (f32[1,25,256]{2,1,0:T(8,128)S(1)}, f32[1,25,256]{2,1,0:T(8,128)S(1)}, u32[]{:S(2)}, u32[]{:S(2)}) collective-permute-start(f32[1,25,256]{2,1,0:T(8,128)S(1)} %get-tuple-element.330), channel_id=1, source_target_pairs={{8,0},{16,8},{24,16},{32,24},{40,32},{48,40},{56,48},{64,56},{72,6... | collective-permute-start | bytes 76808 | tf_op jit(solution)/shard_map/ppermute | solution.py:25
  335.9 2.8 collective-permute-done.23
  338.8 32.9 %while.68 = (s32[]{:T(128)}, f32[12,25,512]{2,1,0:T(8,128)S(1)}, s32[12,512]{1,0:T(8,128)S(1)}, f32[25,3840]{1,0:T(8,128)S(1)}, s32[]{:T(128)}) while((s32[]{:T(128)}, f32[12,25,512]{2,1,0:T(8,128)S(1)}, s32[12,512]{1,0:T(8,128)S(1)}, f32[25,3840]{1,0:T(8,128)S(1)}, s32[]{:T(128)}) %tuple.161), condition=%wide.region_12.13_spmd.clone, body=%wide.region_11.12_spmd.clone.sunk | while | flops 591790080 | bytes 563269 | solution.py:104
  (267 shorter events, 177.4 us)
Async XLA Ops:
  0.6 7.3 %copy-start = (f32[125,1024]{1,0:T(8,128)S(1)}, f32[125,1024]{1,0:T(8,128)}, u32[]{:S(2)}) copy-start(f32[125,1024]{1,0:T(8,128)} %param.19) | copy-start | bytes 1536004
  9.1 1.2 copy-start.1
  9.7 1.3 copy-start.3
  13.7 69.0 %copy-start.4 = (s32[1,768]{1,0:T(1,128)S(1)}, s32[1,768]{1,0:T(1,128)}, u32[]{:S(2)}) copy-start(s32[1,768]{1,0:T(1,128)} %param.25) | copy-start | bytes 9220
  68.5 17.3 %collective-permute-start = (f32[1,50,256]{2,1,0:T(8,128)S(1)}, f32[1,50,256]{2,1,0:T(8,128)S(1)}, u32[]{:S(2)}, u32[]{:S(2)}) collective-permute-start(f32[1,50,256]{2,1,0:T(8,128)S(1)} %get-tuple-element.316), channel_id=1, source_target_pairs={{0,8},{8,16},{16,24},{24,32},{32,40},{40,48},{48,56},{56,64},{64,7... | collective-permute-start | bytes 153608 | tf_op jit(solution)/shard_map/ppermute | solution.py:23
  71.7 14.1 %collective-permute-start.1 = (f32[1,50,256]{2,1,0:T(8,128)S(1)}, f32[1,50,256]{2,1,0:T(8,128)S(1)}, u32[]{:S(2)}, u32[]{:S(2)}) collective-permute-start(f32[1,50,256]{2,1,0:T(8,128)S(1)} %get-tuple-element.317), channel_id=1, source_target_pairs={{8,0},{16,8},{24,16},{32,24},{40,32},{48,40},{56,48},{64,56},{72,6... | collective-permute-start | bytes 153608 | tf_op jit(solution)/shard_map/ppermute | solution.py:25
  75.9 6.8 %collective-permute-start.2 = (f32[1,50,128]{2,1,0:T(8,128)S(1)}, f32[1,50,128]{2,1,0:T(8,128)S(1)}, u32[]{:S(2)}, u32[]{:S(2)}) collective-permute-start(f32[1,50,128]{2,1,0:T(8,128)S(1)} %get-tuple-element.318), channel_id=1, source_target_pairs={{0,1},{1,2},{2,3},{3,4},{4,5},{5,6},{6,7},{8,9},{9,10},{10,11},{11... | collective-permute-start | bytes 76808 | tf_op jit(solution)/shard_map/ppermute | solution.py:23
  80.6 5.2 %collective-permute-start.3 = (f32[1,50,128]{2,1,0:T(8,128)S(1)}, f32[1,50,128]{2,1,0:T(8,128)S(1)}, u32[]{:S(2)}, u32[]{:S(2)}) collective-permute-start(f32[1,50,128]{2,1,0:T(8,128)S(1)} %get-tuple-element.319), channel_id=1, source_target_pairs={{1,0},{2,1},{3,2},{4,3},{5,4},{6,5},{7,6},{9,8},{10,9},{11,10},{12... | collective-permute-start | bytes 76808 | tf_op jit(solution)/shard_map/ppermute | solution.py:25
  89.4 22.1 %copy-start.6 = (f32[25,3072]{1,0:T(8,128)}, f32[25,3072]{1,0:T(8,128)S(1)}, u32[]{:S(2)}) copy-start(f32[25,3072]{1,0:T(8,128)S(1)} %fusion.47) | copy-start | bytes 921604
  92.9 3.5 copy-start.8
  96.5 12.0 %collective-permute-start.4 = (f32[1,25,256]{2,1,0:T(8,128)S(1)}, f32[1,25,256]{2,1,0:T(8,128)S(1)}, u32[]{:S(2)}, u32[]{:S(2)}) collective-permute-start(f32[1,25,256]{2,1,0:T(8,128)S(1)} %get-tuple-element.339), channel_id=1, source_target_pairs={{0,8},{8,16},{16,24},{24,32},{32,40},{40,48},{48,56},{56,64},{64,7... | collective-permute-start | bytes 76808 | tf_op jit(solution)/shard_map/ppermute | solution.py:23
  98.4 10.1 %collective-permute-start.5 = (f32[1,25,256]{2,1,0:T(8,128)S(1)}, f32[1,25,256]{2,1,0:T(8,128)S(1)}, u32[]{:S(2)}, u32[]{:S(2)}) collective-permute-start(f32[1,25,256]{2,1,0:T(8,128)S(1)} %get-tuple-element.338), channel_id=1, source_target_pairs={{8,0},{16,8},{24,16},{32,24},{40,32},{48,40},{56,48},{64,56},{72,6... | collective-permute-start | bytes 76808 | tf_op jit(solution)/shard_map/ppermute | solution.py:25
  103.9 4.7 %collective-permute-start.6 = (f32[1,25,128]{2,1,0:T(8,128)S(1)}, f32[1,25,128]{2,1,0:T(8,128)S(1)}, u32[]{:S(2)}, u32[]{:S(2)}) collective-permute-start(f32[1,25,128]{2,1,0:T(8,128)S(1)} %get-tuple-element.337), channel_id=1, source_target_pairs={{0,1},{1,2},{2,3},{3,4},{4,5},{5,6},{6,7},{8,9},{9,10},{10,11},{11... | collective-permute-start | bytes 38408 | tf_op jit(solution)/shard_map/ppermute | solution.py:23
  106.4 5.1 %collective-permute-start.7 = (f32[1,25,128]{2,1,0:T(8,128)S(1)}, f32[1,25,128]{2,1,0:T(8,128)S(1)}, u32[]{:S(2)}, u32[]{:S(2)}) collective-permute-start(f32[1,25,128]{2,1,0:T(8,128)S(1)} %get-tuple-element.336), channel_id=1, source_target_pairs={{1,0},{2,1},{3,2},{4,3},{5,4},{6,5},{7,6},{9,8},{10,9},{11,10},{12... | collective-permute-start | bytes 38408 | tf_op jit(solution)/shard_map/ppermute | solution.py:25
  186.8 15.0 %collective-permute-start.8 = (f32[1,25,256]{2,1,0:T(8,128)S(1)}, f32[1,25,256]{2,1,0:T(8,128)S(1)}, u32[]{:S(2)}, u32[]{:S(2)}) collective-permute-start(f32[1,25,256]{2,1,0:T(8,128)S(1)} %get-tuple-element.324), channel_id=1, source_target_pairs={{0,8},{8,16},{16,24},{24,32},{32,40},{40,48},{48,56},{56,64},{64,7... | collective-permute-start | bytes 76808 | tf_op jit(solution)/shard_map/ppermute | solution.py:23
  188.7 13.1 %collective-permute-start.9 = (f32[1,25,256]{2,1,0:T(8,128)S(1)}, f32[1,25,256]{2,1,0:T(8,128)S(1)}, u32[]{:S(2)}, u32[]{:S(2)}) collective-permute-start(f32[1,25,256]{2,1,0:T(8,128)S(1)} %get-tuple-element.325), channel_id=1, source_target_pairs={{8,0},{16,8},{24,16},{32,24},{40,32},{48,40},{56,48},{64,56},{72,6... | collective-permute-start | bytes 76808 | tf_op jit(solution)/shard_map/ppermute | solution.py:25
  194.2 4.9 %collective-permute-start.10 = (f32[1,25,128]{2,1,0:T(8,128)S(1)}, f32[1,25,128]{2,1,0:T(8,128)S(1)}, u32[]{:S(2)}, u32[]{:S(2)}) collective-permute-start(f32[1,25,128]{2,1,0:T(8,128)S(1)} %get-tuple-element.326), channel_id=1, source_target_pairs={{0,1},{1,2},{2,3},{3,4},{4,5},{5,6},{6,7},{8,9},{9,10},{10,11},{11... | collective-permute-start | bytes 38408 | tf_op jit(solution)/shard_map/ppermute | solution.py:23
  196.7 5.1 %collective-permute-start.11 = (f32[1,25,128]{2,1,0:T(8,128)S(1)}, f32[1,25,128]{2,1,0:T(8,128)S(1)}, u32[]{:S(2)}, u32[]{:S(2)}) collective-permute-start(f32[1,25,128]{2,1,0:T(8,128)S(1)} %get-tuple-element.327), channel_id=1, source_target_pairs={{1,0},{2,1},{3,2},{4,3},{5,4},{6,5},{7,6},{9,8},{10,9},{11,10},{12... | collective-permute-start | bytes 38408 | tf_op jit(solution)/shard_map/ppermute | solution.py:25
  206.4 18.4 %copy-start.7 = (f32[25,3072]{1,0:T(8,128)}, f32[25,3072]{1,0:T(8,128)S(1)}, u32[]{:S(2)}) copy-start(f32[25,3072]{1,0:T(8,128)S(1)} %get-tuple-element.351) | copy-start | bytes 921604
  209.9 12.0 %collective-permute-start.12 = (f32[1,25,256]{2,1,0:T(8,128)S(1)}, f32[1,25,256]{2,1,0:T(8,128)S(1)}, u32[]{:S(2)}, u32[]{:S(2)}) collective-permute-start(f32[1,25,256]{2,1,0:T(8,128)S(1)} %get-tuple-element.335), channel_id=1, source_target_pairs={{0,8},{8,16},{16,24},{24,32},{32,40},{40,48},{48,56},{56,64},{64,7... | collective-permute-start | bytes 76808 | tf_op jit(solution)/shard_map/ppermute | solution.py:23
  211.8 10.1 %collective-permute-start.13 = (f32[1,25,256]{2,1,0:T(8,128)S(1)}, f32[1,25,256]{2,1,0:T(8,128)S(1)}, u32[]{:S(2)}, u32[]{:S(2)}) collective-permute-start(f32[1,25,256]{2,1,0:T(8,128)S(1)} %get-tuple-element.334), channel_id=1, source_target_pairs={{8,0},{16,8},{24,16},{32,24},{40,32},{48,40},{56,48},{64,56},{72,6... | collective-permute-start | bytes 76808 | tf_op jit(solution)/shard_map/ppermute | solution.py:25
  217.3 4.7 %collective-permute-start.14 = (f32[1,25,128]{2,1,0:T(8,128)S(1)}, f32[1,25,128]{2,1,0:T(8,128)S(1)}, u32[]{:S(2)}, u32[]{:S(2)}) collective-permute-start(f32[1,25,128]{2,1,0:T(8,128)S(1)} %get-tuple-element.333), channel_id=1, source_target_pairs={{0,1},{1,2},{2,3},{3,4},{4,5},{5,6},{6,7},{8,9},{9,10},{10,11},{11... | collective-permute-start | bytes 38408 | tf_op jit(solution)/shard_map/ppermute | solution.py:23
  219.8 5.1 %collective-permute-start.15 = (f32[1,25,128]{2,1,0:T(8,128)S(1)}, f32[1,25,128]{2,1,0:T(8,128)S(1)}, u32[]{:S(2)}, u32[]{:S(2)}) collective-permute-start(f32[1,25,128]{2,1,0:T(8,128)S(1)} %get-tuple-element.332), channel_id=1, source_target_pairs={{1,0},{2,1},{3,2},{4,3},{5,4},{6,5},{7,6},{9,8},{10,9},{11,10},{12... | collective-permute-start | bytes 38408 | tf_op jit(solution)/shard_map/ppermute | solution.py:25
  262.9 1.0 copy-start.2
  300.4 15.0 %collective-permute-start.16 = (f32[1,25,256]{2,1,0:T(8,128)S(1)}, f32[1,25,256]{2,1,0:T(8,128)S(1)}, u32[]{:S(2)}, u32[]{:S(2)}) collective-permute-start(f32[1,25,256]{2,1,0:T(8,128)S(1)} %get-tuple-element.320), channel_id=1, source_target_pairs={{0,8},{8,16},{16,24},{24,32},{32,40},{40,48},{48,56},{56,64},{64,7... | collective-permute-start | bytes 76808 | tf_op jit(solution)/shard_map/ppermute | solution.py:23
  302.4 13.1 %collective-permute-start.17 = (f32[1,25,256]{2,1,0:T(8,128)S(1)}, f32[1,25,256]{2,1,0:T(8,128)S(1)}, u32[]{:S(2)}, u32[]{:S(2)}) collective-permute-start(f32[1,25,256]{2,1,0:T(8,128)S(1)} %get-tuple-element.321), channel_id=1, source_target_pairs={{8,0},{16,8},{24,16},{32,24},{40,32},{48,40},{56,48},{64,56},{72,6... | collective-permute-start | bytes 76808 | tf_op jit(solution)/shard_map/ppermute | solution.py:25
  307.9 4.6 %collective-permute-start.18 = (f32[1,25,128]{2,1,0:T(8,128)S(1)}, f32[1,25,128]{2,1,0:T(8,128)S(1)}, u32[]{:S(2)}, u32[]{:S(2)}) collective-permute-start(f32[1,25,128]{2,1,0:T(8,128)S(1)} %get-tuple-element.322), channel_id=1, source_target_pairs={{0,1},{1,2},{2,3},{3,4},{4,5},{5,6},{6,7},{8,9},{9,10},{10,11},{11... | collective-permute-start | bytes 38408 | tf_op jit(solution)/shard_map/ppermute | solution.py:23
  310.4 5.1 %collective-permute-start.19 = (f32[1,25,128]{2,1,0:T(8,128)S(1)}, f32[1,25,128]{2,1,0:T(8,128)S(1)}, u32[]{:S(2)}, u32[]{:S(2)}) collective-permute-start(f32[1,25,128]{2,1,0:T(8,128)S(1)} %get-tuple-element.323), channel_id=1, source_target_pairs={{1,0},{2,1},{3,2},{4,3},{5,4},{6,5},{7,6},{9,8},{10,9},{11,10},{12... | collective-permute-start | bytes 38408 | tf_op jit(solution)/shard_map/ppermute | solution.py:25
  320.2 18.5 %copy-start.5 = (f32[25,3072]{1,0:T(8,128)}, f32[25,3072]{1,0:T(8,128)S(1)}, u32[]{:S(2)}) copy-start(f32[25,3072]{1,0:T(8,128)S(1)} %get-tuple-element.353) | copy-start | bytes 921604
  323.7 12.1 %collective-permute-start.20 = (f32[1,25,256]{2,1,0:T(8,128)S(1)}, f32[1,25,256]{2,1,0:T(8,128)S(1)}, u32[]{:S(2)}, u32[]{:S(2)}) collective-permute-start(f32[1,25,256]{2,1,0:T(8,128)S(1)} %get-tuple-element.331), channel_id=1, source_target_pairs={{0,8},{8,16},{16,24},{24,32},{32,40},{40,48},{48,56},{56,64},{64,7... | collective-permute-start | bytes 76808 | tf_op jit(solution)/shard_map/ppermute | solution.py:23
  325.6 10.2 %collective-permute-start.21 = (f32[1,25,256]{2,1,0:T(8,128)S(1)}, f32[1,25,256]{2,1,0:T(8,128)S(1)}, u32[]{:S(2)}, u32[]{:S(2)}) collective-permute-start(f32[1,25,256]{2,1,0:T(8,128)S(1)} %get-tuple-element.330), channel_id=1, source_target_pairs={{8,0},{16,8},{24,16},{32,24},{40,32},{48,40},{56,48},{64,56},{72,6... | collective-permute-start | bytes 76808 | tf_op jit(solution)/shard_map/ppermute | solution.py:25
  331.1 4.7 %collective-permute-start.22 = (f32[1,25,128]{2,1,0:T(8,128)S(1)}, f32[1,25,128]{2,1,0:T(8,128)S(1)}, u32[]{:S(2)}, u32[]{:S(2)}) collective-permute-start(f32[1,25,128]{2,1,0:T(8,128)S(1)} %get-tuple-element.329), channel_id=1, source_target_pairs={{0,1},{1,2},{2,3},{3,4},{4,5},{5,6},{6,7},{8,9},{9,10},{10,11},{11... | collective-permute-start | bytes 38408 | tf_op jit(solution)/shard_map/ppermute | solution.py:23
  333.6 5.1 %collective-permute-start.23 = (f32[1,25,128]{2,1,0:T(8,128)S(1)}, f32[1,25,128]{2,1,0:T(8,128)S(1)}, u32[]{:S(2)}, u32[]{:S(2)}) collective-permute-start(f32[1,25,128]{2,1,0:T(8,128)S(1)} %get-tuple-element.328), channel_id=1, source_target_pairs={{1,0},{2,1},{3,2},{4,3},{5,4},{6,5},{7,6},{9,8},{10,9},{11,10},{12... | collective-permute-start | bytes 38408 | tf_op jit(solution)/shard_map/ppermute | solution.py:25
where the time goes:
time: 385 us; the launch traced here: 378 us
  matrix products  254 us (66%)
  starting transfers between devices  74.4 us (19%)
  local copies, waits for them, and re-layouts  24.3 us (6%)
  waiting for transfers between devices  17.2 us (4%)
    dot_general x36, matrix products, add_block(): jnp.dot(term_block, selector, precision=HIGH, preferred_element_type=jnp....  110 us
    dot_general x36, matrix products, take_block(): jnp.dot(trace_table, selector, precision=HIGH, preferred_element_type=jnp...  97.8 us
    ppermute x12, starting transfers between devices, with_halo(): lax.ppermute(head, axis, [((i + 1) % count, i) for i in range(ends)])  44.5 us
    ppermute x12, starting transfers between devices, with_halo(): lax.ppermute(tail, axis, [(i, (i + 1) % count) for i in range(ends)])  29.9 us
    ppermute x12, waiting for transfers between devices, with_halo(): lax.ppermute(head, axis, [((i + 1) % count, i) for i in range(ends)])  17.2 us
    dynamic_slice x108, local copies, waits for them, and re-layouts, assemble(): lax.scan(add_block, jnp.zeros((row_count, table_width), jnp.float32), (te...  17 us
    dot_general x4, matrix products, add_arrivals(): jnp.dot(arrived, selector, precision=HIGH, preferred_element_type=jnp.flo...  16.5 us
    dot_general x16, matrix products, per_material(): jnp.dot(inverses[mat_id], values, precision=HIGH, preferred_element_type=...  10.6 us
  transfers between devices with their start and end apart: 24, of which 6 were waited for; matrix products, arithmetic and copies ran while one was open for 0% of the time, Pallas kernels for 0%

commit v1 on v0

v1 whole, which is shorter than its diff:
```python
import functools

import jax
import jax.numpy as jnp
from jax import lax
from jax.experimental import pallas as pl
from jax.experimental.pallas import tpu as pltpu
from jax.sharding import PartitionSpec as P

MESH = pl.DeviceIdType.MESH
F32, BF = jnp.float32, jnp.bfloat16
HIGH = lax.Precision.HIGHEST
DAMPING = 0.6
SWEEPS = 3

NODES, FNODES, SIDES, MATS = 125, 25, 6, 4
ELEM = 1024
OWNED = 3 * ELEM
CAP_W, CAP_N = 256, 128
GHOSTS = 2 * CAP_W + 2 * CAP_N
TP = 160
NP = 128

OWN_BLOCKS, BLOCKS = 12, 18
OWN_MAIN, OWN_LEFT, OUT_MAIN, OUT_LEFT, ROWS = 0, 288, 304, 448, 464
GROUPS = {
    "own": (0, 12, OWN_MAIN, OWN_LEFT),
    "out": (12, 18, OUT_MAIN, OUT_LEFT),
}
SENT = 56
ROUNDS = 2 + SWEEPS - 1


def dot(a, b, precision=None):
    return jnp.dot(a, b, precision=precision, preferred_element_type=F32)


def dot_nt(a, b, precision=None):
    return lax.dot_general(
        a, b, (((1,), (1,)), ((), ())), precision=precision, preferred_element_type=F32
    )


def split(x):
    hi = x.astype(BF)
    return hi, (x - hi.astype(F32)).astype(BF)


def iota(shape, dim):
    return lax.broadcasted_iota(jnp.int32, shape, dim)


def trace_position(p):
    side = jnp.zeros_like(p)
    for i in range(1, SIDES):
        side = side + (p >= 24 * i).astype(jnp.int32)
    node = jnp.where(p < 144, p - 24 * side, 24)
    side = jnp.where(p < 144, side, p - 144)
    return side, node


def kernel(
    source, inverses, lift, stab, material, face_slot, owner_map,
    potential, trace_own,
    onehot, onehot_out, blk_f, blk_d, idx_f, counts,
    inv_pad, lift_pad, src_pad, src3, left3, a3, w3,
    rhs_terms, x_main, x_left, x3, t_hi, t_lo, l_hi, l_lo,
    partial, total, table, table2, scale,
    send_w, recv_w, send_n, recv_n, send_sems, recv_sems,
):
    w, n = lax.axis_index("wide"), lax.axis_index("narrow")
    wide, narrow = lax.axis_size("wide"), lax.axis_size("narrow")
    there = (w > 0, w < wide - 1, n > 0, n < narrow - 1)
    neighbour = ((w - 1, n), (w + 1, n), (w, n - 1), (w, n + 1))
    barrier = pltpu.get_barrier_semaphore()
    present = jnp.int32(0)
    for k in range(4):
        present = present + there[k].astype(jnp.int32)

        @pl.when(there[k])
        def _():
            pl.semaphore_signal(barrier, inc=1, device_id=neighbour[k], device_id_type=MESH)

    pl.semaphore_wait(barrier, present)

    def buffers(k):
        return (send_w, recv_w, k) if k < 2 else (send_n, recv_n, k - 2)

    for k in range(4):
        send, recv, side = buffers(k)

        @pl.when(jnp.logical_not(there[k]))
        def _():
            for r in range(ROUNDS):
                recv[r, side] = jnp.zeros(recv.shape[2:], F32)

    def copy(r, k):
        send, recv, side = buffers(k)
        return pltpu.make_async_remote_copy(
            src_ref=send.at[r, side],
            dst_ref=recv.at[r, 1 - side],
            send_sem=send_sems.at[r, k],
            recv_sem=recv_sems.at[r, k ^ 1],
            device_id=neighbour[k],
            device_id_type=MESH,
        )

    def arrival(r, k):
        send, recv, side = buffers(k)
        return pltpu.make_async_remote_copy(
            src_ref=send.at[r, side],
            dst_ref=recv.at[r, side],
            send_sem=send_sems.at[r, k],
            recv_sem=recv_sems.at[r, k],
            device_id=neighbour[k],
            device_id_type=MESH,
        )

    def places(k):
        block = min(k, 2)
        lo, width = (0, CAP_W) if k < 2 else ((k - 2) * CAP_N, CAP_N)
        return block, slice(lo, lo + width)

    def post(r, values):
        for k in range(4):
            send, recv, side = buffers(k)
            block, cols = places(k)
            ghost, shared = OUT_MAIN + 24 * block, OUT_MAIN + 24 * (block + 3)
            send[r, side, 0:24] = values[ghost : ghost + 24, cols]
            send[r, side, 24:48] = values[shared : shared + 24, cols]
            ghost, shared = OUT_LEFT + block, OUT_LEFT + block + 3
            send[r, side, 48:49] = values[ghost : ghost + 1, cols]
            send[r, side, 49:50] = values[shared : shared + 1, cols]

            @pl.when(there[k])
            def _():
                copy(r, k).start()

    def collect(r, values):
        for k in range(4):
            @pl.when(there[k])
            def _():
                arrival(r, k).wait_recv()

        for k in range(4):
            send, recv, side = buffers(k)
            block, cols = places(k)
            ghost, shared = OUT_MAIN + 24 * block, OUT_MAIN + 24 * (block + 3)
            values[shared : shared + 24, cols] += recv[r, side, 0:24]
            values[ghost : ghost + 24, cols] += recv[r, side, 24:48]
            ghost, shared = OUT_LEFT + block, OUT_LEFT + block + 3
            values[shared : shared + 1, cols] += recv[r, side, 48:49]
            values[ghost : ghost + 1, cols] += recv[r, side, 49:50]

    owners = owner_map[...]
    own_blk, own_col = owners >> 8, owners & 255
    place = iota((1, GHOSTS), 1) + 1
    onehot_out[...] = (iota((256, GHOSTS), 0) == own_col).astype(F32).astype(BF)
    row16 = iota((16, GHOSTS), 0)
    named = jnp.where(row16 < OWN_BLOCKS, row16, -1) == own_blk
    digits = jnp.concatenate(
        [
            jnp.where(named, (place >> 8).astype(F32), 0.0),
            jnp.where(named, (place & 255).astype(F32), 0.0),
        ],
        axis=0,
    ).astype(BF)
    place_table = dot_nt(digits, onehot_out[...]).astype(BF)

    def renumber(s, carry):
        v = face_slot[pl.ds(s, 1), :]
        col = jnp.broadcast_to(v & 255, (256, ELEM))
        first = (iota((256, ELEM), 0) == col).astype(F32).astype(BF)
        found = dot(place_table, first)
        hit = iota((16, ELEM), 0) == (v >> 8)
        spot = jnp.sum(
            jnp.where(hit, 256.0 * found[0:16] + found[16:32], 0.0), axis=0, keepdims=True
        ).astype(jnp.int32)
        v = jnp.where(spot > 0, OWNED + GHOSTS - 1 + spot, v)
        onehot[s] = (iota((256, ELEM), 0) == (v & 255)).astype(F32).astype(BF)
        blk = (v >> 8).astype(F32)
        blk_f[s] = jnp.broadcast_to(blk, (8, ELEM))
        blk_d[s] = (blk - (iota((48, ELEM), 0) >= 24).astype(F32)).astype(BF)
        idx = 8.0 * blk + material[...].astype(F32)
        idx_f[s] = (idx - iota((16, ELEM), 0).astype(F32)).astype(BF)
        return carry

    lax.fori_loop(0, SIDES, renumber, 0)

    def count(s, carry):
        idx = idx_f[s]
        ones = jnp.concatenate(
            [
                jnp.where(idx == BF(16 * t), BF(1), BF(0))
                for t in range(8 * BLOCKS // 16)
            ],
            axis=0,
        )
        counts[s] = dot_nt(ones, onehot[s])
        return carry

    lax.fori_loop(0, SIDES, count, 0)

    inv_pad[...] = jnp.zeros_like(inv_pad)
    inv_pad[:, 0:NODES, 0:NODES] = inverses[...]
    lift_pad[...] = jnp.zeros_like(lift_pad)
    lift_pad[0:NODES, 0 : SIDES * FNODES] = lift[...]
    src_pad[...] = jnp.zeros_like(src_pad)
    src_pad[0:NODES] = source[...]
    hi, lo = split(src_pad[...])
    src3[0:NP], src3[NP : 2 * NP], src3[2 * NP :] = hi, lo, hi

    side_p, node_p = trace_position(iota((TP, 256), 0))
    order = jnp.where(side_p < SIDES, 6 * node_p + side_p, -1)
    perm = (iota((TP, 256), 1) == order).astype(F32)
    lift_t = dot_nt(perm, lift_pad[...], HIGH)
    lift_p = dot_nt(lift_pad[...], perm, HIGH)
    eye = iota((TP, TP), 0) == iota((TP, TP), 1)
    col = iota((TP, 192), 1)
    for i in range(1, 4):
        col = col - 48 * (iota((TP, 192), 1) >= 48 * i).astype(jnp.int32)
    side_c, _ = trace_position(iota((TP, 192), 0))
    spread = jnp.zeros((TP, 192), F32)
    for m in range(MATS):
        inv = inv_pad[m]
        wm = dot(inv, lift_p, HIGH)
        wt = dot(lift_t, inv, HIGH)
        am = dot(wt, lift_p, HIGH)
        diagonal = jnp.abs(jnp.sum(jnp.where(eye, am, 0.0), axis=1, keepdims=True)) + stab[m]
        spread = spread + jnp.where(col == 8 * side_c + m, diagonal, 0.0)
        am = am + jnp.where(eye, stab[m], 0.0)
        hi, lo = split(am)
        a3[TP * m : TP * (m + 1)] = jnp.concatenate([hi, hi, lo], axis=1)
        hi, lo = split(wm)
        w3[NP * m : NP * (m + 1)] = jnp.concatenate([hi, hi, lo], axis=1)
        hi, lo = split(wt)
        r = slice(TP * m, TP * (m + 1))
        left3[r, 0:NP], left3[r, NP : 2 * NP], left3[r, 2 * NP :] = hi, hi, lo
        hi, lo = split(inv)
        r = slice(MATS * TP + NP * m, MATS * TP + NP * (m + 1))
        left3[r, 0:NP], left3[r, NP : 2 * NP], left3[r, 2 * NP :] = hi, hi, lo
    sdiag = jnp.zeros((24, 192), F32)
    for s in range(SIDES):
        sdiag = sdiag + spread[24 * s : 24 * s + 24]
    last = jnp.sum(spread[144:152], axis=0, keepdims=True)
    sdiag = jnp.concatenate([sdiag, jnp.broadcast_to(last, (8, 192))], axis=0)
    hi = sdiag.astype(BF).astype(F32)
    sdiag = jnp.where(iota((32, 192), 1) < 96, hi, sdiag - hi).astype(BF)

    def diag_block(a):
        _, _, main, left = GROUPS["own" if a < OWN_BLOCKS else "out"]
        b = a if a < OWN_BLOCKS else a - OWN_BLOCKS
        met = jnp.concatenate([counts[s, 8 * a : 8 * a + 8] for s in range(SIDES)], axis=0)
        hi, lo = split(met)
        d = dot(sdiag, jnp.concatenate([hi, lo, hi, lo], axis=0))
        scale[main + 24 * b : main + 24 * b + 24] = d[0:24]
        scale[left + b : left + b + 1] = d[24:25]

    scale[...] = jnp.zeros_like(scale)
    for a in range(OWN_BLOCKS, BLOCKS):
        diag_block(a)
    post(0, scale)

    mat = material[...]

    def pick(y, width, e):
        m_row = jnp.broadcast_to(mat[:, e], (8, y.shape[1]))[None]
        y = y.reshape(MATS, width // 8, 8, y.shape[1])
        return jnp.where(
            m_row == 0, y[0], jnp.where(m_row == 1, y[1], jnp.where(m_row == 2, y[2], y[3]))
        ).reshape(width, y.shape[3])

    CHUNK = 512
    for c in range(ELEM // CHUNK):
        e = slice(c * CHUNK, (c + 1) * CHUNK)
        y = dot(left3[...], src3[:, e])
        rhs_terms[:, e] = pick(y[0 : MATS * TP], TP, e)
        potential[:, e] = pick(y[MATS * TP :], NP, e)[0:NODES]

    def store_terms(terms, e):
        for s in range(SIDES):
            t = terms[24 * s : 24 * s + 24]
            hi, lo = split(jnp.concatenate([t, t], axis=0))
            t_hi[s, :, e], t_lo[s, :, e] = hi, lo
            t = jnp.broadcast_to(terms[144 + s : 145 + s], (16, terms.shape[1]))
            hi, lo = split(t)
            l_hi[s, :, e], l_lo[s, :, e] = hi, lo

    for c in range(ELEM // CHUNK):
        e = slice(c * CHUNK, (c + 1) * CHUNK)
        store_terms(rhs_terms[:, e], e)

    def row_ids(first, last, dtype):
        r = iota((16, ELEM), 0)
        return jnp.where(r < last - first, r + first, -1).astype(F32).astype(dtype)

    def assemble(name):
        first, last, main, left = GROUPS[name]
        rows = slice(main, left + 16)
        partial[rows] = jnp.zeros((left + 16 - main, 256), F32)

        def add(s, carry):
            hit = row_ids(first, last, BF) == blk_d[s, 0:16]
            hits = [blk_d[s] == BF(a) for a in range(first, last, 2)]
            out = None
            for t, l in ((t_hi, l_hi), (t_lo, l_lo)):
                tv = t[s]
                z = jnp.concatenate(
                    [jnp.where(h, tv, BF(0)) for h in hits] + [jnp.where(hit, l[s], BF(0))], axis=0
                )
                d = dot_nt(z, onehot[s])
                out = d if out is None else out + d
            partial[rows] += out
            return carry

        lax.fori_loop(0, SIDES, add, 0)

    def fetch(name):
        first, last, main, left = GROUPS[name]

        def take(s, carry):
            y = dot(table[main : left + 16], onehot[s]) + dot(table2[main : left + 16], onehot[s])
            blk = blk_f[s]
            if name == "own":
                acc = jnp.zeros((3, 8, ELEM), F32)
                acc_left = jnp.zeros((1, ELEM), F32)
            else:
                acc = x_main[s].reshape(3, 8, ELEM)
                acc_left = x_left[s, 0:1]
            for a in range(first, last):
                ya = y[24 * (a - first) : 24 * (a - first) + 24].reshape(3, 8, ELEM)
                acc = jnp.where((blk == F32(a))[None], ya, acc)
            x_main[s] = acc.reshape(24, ELEM)
            hit = row_ids(first, last, F32).reshape(2, 8, ELEM) == blk[None]
            yl = jnp.where(hit, y[left - main :].reshape(2, 8, ELEM), 0.0)
            x_left[s, 0:1] = acc_left + jnp.sum(yl[0] + yl[1], axis=0, keepdims=True)
            return carry

        lax.fori_loop(0, SIDES, take, 0)

    def gathered():
        rows = [x_main[s] for s in range(SIDES)]
        x = jnp.concatenate([x_left[s, 0:1] for s in range(SIDES)] + [jnp.zeros((10, ELEM), F32)], axis=0)
        x = jnp.concatenate(rows + [x], axis=0)
        hi, lo = split(x)
        x3[0:TP], x3[TP : 2 * TP], x3[2 * TP :] = hi, lo, hi

    def table_rows(name):
        _, _, main, left = GROUPS[name]
        return slice(main, left + 16)

    def update(name, first):
        rows = table_rows(name)
        step = scale[rows] * partial[rows]
        x = step if first else total[rows] + step
        total[rows] = x
        hi, lo = split(x)
        table[rows], table2[rows] = hi, lo

    assemble("out")
    post(1, partial)
    for a in range(OWN_BLOCKS):
        diag_block(a)
    assemble("own")

    def invert(name):
        rows = table_rows(name)
        d = scale[rows]
        scale[rows] = jnp.where(d == 0.0, 0.0, DAMPING / jnp.where(d == 0.0, 1.0, d))

    invert("own")
    update("own", True)
    fetch("own")
    collect(0, scale)
    collect(1, partial)
    invert("out")
    update("out", True)
    fetch("out")

    for sweep in range(SWEEPS - 1):
        gathered()
        for c in range(ELEM // CHUNK):
            e = slice(c * CHUNK, (c + 1) * CHUNK)
            y = pick(dot(a3[...], x3[:, e]), TP, e)
            store_terms(rhs_terms[:, e] - y, e)
        assemble("out")
        post(2 + sweep, partial)
        assemble("own")
        update("own", False)
        fetch("own")
        collect(2 + sweep, partial)
        update("out", False)
        fetch("out")

    rows = slice(OWN_MAIN, OWN_LEFT + 16)
    back = jnp.zeros((304, 256), F32)
    for b in range(3):
        cols = slice(256 * b, 256 * (b + 1))
        r = OUT_MAIN + 24 * (b + 3)
        x = total[r : r + 24]
        xl = jnp.broadcast_to(total[OUT_LEFT + b + 3 : OUT_LEFT + b + 4], (16, 256))
        blk = own_blk[:, cols].astype(F32)
        blk2 = (blk - (iota((48, 256), 0) >= 24).astype(F32)).astype(BF)
        hits = [blk2 == BF(a) for a in range(0, OWN_BLOCKS, 2)]
        r16 = iota((16, 256), 0)
        hit = jnp.where(r16 < OWN_BLOCKS, r16, -1).astype(F32).astype(BF) == blk.astype(BF)
        for xv, lv in zip(split(jnp.concatenate([x, x], axis=0)), split(xl)):
            z = jnp.concatenate(
                [jnp.where(h, xv, BF(0)) for h in hits] + [jnp.where(hit, lv, BF(0))], axis=0
            )
            back = back + dot_nt(z, onehot_out[:, cols])
    full = total[rows] + back
    for a in range(OWN_BLOCKS):
        cols = slice(256 * a, 256 * (a + 1))
        trace_own[0:24, cols] = full[24 * a : 24 * a + 24]
        trace_own[24:25, cols] = full[OWN_LEFT + a : OWN_LEFT + a + 1]

    gathered()
    for c in range(ELEM // CHUNK):
        e = slice(c * CHUNK, (c + 1) * CHUNK)
        y = pick(dot(w3[...], x3[:, e]), NP, e)
        potential[:, e] = potential[:, e] - y[0:NODES]

    for r in range(ROUNDS):
        for k in range(4):
            @pl.when(there[k])
            def _():
                copy(r, k).wait_send()


def shards(source, inverses, lift, stab, material, face_slot, owner_map):
    vmem = pl.BlockSpec(memory_space=pltpu.VMEM)
    smem = pl.BlockSpec(memory_space=pltpu.SMEM)
    v = pltpu.VMEM
    return pl.pallas_call(
        kernel,
        out_shape=(
            jax.ShapeDtypeStruct((NODES, ELEM), F32),
            jax.ShapeDtypeStruct((FNODES, OWNED), F32),
        ),
        in_specs=[vmem, vmem, vmem, smem, vmem, vmem, vmem],
        out_specs=(vmem, vmem),
        scratch_shapes=[
            v((SIDES, 256, ELEM), BF),
            v((256, GHOSTS), BF),
            v((SIDES, 8, ELEM), F32),
            v((SIDES, 48, ELEM), BF),
            v((SIDES, 16, ELEM), BF),
            v((SIDES, 8 * BLOCKS, 256), F32),
            v((MATS, NP, NP), F32),
            v((NP, 256), F32),
            v((NP, ELEM), F32),
            v((3 * NP, ELEM), BF),
            v((MATS * (TP + NP), 3 * NP), BF),
            v((MATS * TP, 3 * TP), BF),
            v((MATS * NP, 3 * TP), BF),
            v((TP, ELEM), F32),
            v((SIDES, 24, ELEM), F32),
            v((SIDES, 8, ELEM), F32),
            v((3 * TP, ELEM), BF),
            v((SIDES, 48, ELEM), BF),
            v((SIDES, 48, ELEM), BF),
            v((SIDES, 16, ELEM), BF),
            v((SIDES, 16, ELEM), BF),
            v((ROWS, 256), F32),
            v((ROWS, 256), F32),
            v((ROWS, 256), BF),
            v((ROWS, 256), BF),
            v((ROWS, 256), F32),
            v((ROUNDS, 2, SENT, CAP_W), F32),
            v((ROUNDS, 2, SENT, CAP_W), F32),
            v((ROUNDS, 2, SENT, CAP_N), F32),
            v((ROUNDS, 2, SENT, CAP_N), F32),
            pltpu.SemaphoreType.DMA((ROUNDS, 4)),
            pltpu.SemaphoreType.DMA((ROUNDS, 4)),
        ],
        compiler_params=pltpu.CompilerParams(
            collective_id=0, has_side_effects=True, vmem_limit_bytes=48 * 2**20
        ),
    )(source, inverses, lift, stab, material.reshape(1, ELEM), face_slot, owner_map)


def solution(mesh):
    both = ("wide", "narrow")
    return jax.shard_map(
        shards,
        mesh=mesh,
        in_specs=(
            P(None, both), P(), P(), P(), P(both), P(None, both), P(both, None),
        ),
        out_specs=(P(None, both), P(None, both)),
        check_vma=False,
    )
```

time: 385 us -> 55.9 us (0.15); the launches traced: 378 us -> 55.5 us
  matrix products: 254 us -> 0 us
  starting transfers between devices: 74.4 us -> 0 us
  Pallas kernels: 0 us -> 51.1 us
  local copies, waits for them, and re-layouts: 24.3 us -> 3.62 us
  waiting for transfers between devices: 17.2 us -> 0 us
    dot_general x102 -> x0, matrix products: 254 us -> none  [the longest x36 110 us: add_block(): jnp.dot(term_block, selector, precision=HIGH, preferred_element_type=jnp....]
    ppermute x24 -> x0, starting transfers between devices: 74.4 us -> none  [the longest x12 44.5 us: with_halo(): lax.ppermute(head, axis, [((i + 1) % count, i) for i in range(ends)])]
    pallas_call x0 -> x1, Pallas kernels: none -> 51.1 us  [shards(): pl.pallas_call(kernel, out_shape=(jax.ShapeDtypeStruct((NODES, ELEM), F32...]
    ppermute x24 -> x0, waiting for transfers between devices: 17.2 us -> none  [the longest x12 17.2 us: with_halo(): lax.ppermute(head, axis, [((i + 1) % count, i) for i in range(ends)])]
    dynamic_slice x108 -> x0, local copies, waits for them, and re-layouts: 17 us -> none  [assemble(): lax.scan(add_block, jnp.zeros((row_count, table_width), jnp.float32), (te...]
  transfers between devices with their start and end apart: 24 -> 0, of which waited for: 6 -> 0; matrix products, arithmetic and copies ran while one was open for 0% -> 0% of each run, Pallas kernels for 0% -> 0%
where the time goes in v1:
time: 55.9 us; the launch traced here: 55.5 us
  Pallas kernels  51.1 us (91%)
  local copies, waits for them, and re-layouts  3.62 us (6%)
  between operations  0.72 us (1%)
    pallas_call x1, Pallas kernels, shards(): pl.pallas_call(kernel, out_shape=(jax.ShapeDtypeStruct((NODES, ELEM), F32...  51.1 us
    unnamed x14, local copies, waits for them, and re-layouts  3.62 us

profile of v1, /device:TPU:7, one launch (start us, length us, event | category | flops | bytes accessed | tf_op | source)
XLA Modules:
  0.0 55.5 jit_solution(18085519118566371566)
XLA Ops:
  0.6 0.0 copy-start
  0.6 1.1 %copy.10.lift = f32[125,150]{1,0:T(8,128)S(1)} copy(f32[125,150]{0,1:T(8,128)} %param.9) | data formatting | bytes 150000 | tf_op args[2]
  1.7 0.0 copy-start.1
  1.7 0.0 copy-start.2
  1.7 0.0 copy-start.3
  1.7 0.0 copy-start.4
  1.7 1.0 %copy.9.inverses = f32[4,125,125]{2,1,0:T(8,128)S(1)} copy(f32[4,125,125]{2,0,1:T(4,128)} %param.8) | data formatting | bytes 500000 | tf_op args[1]
  2.7 0.0 copy-done
  2.7 0.0 copy-done.1
  2.8 0.0 copy-done.2
  2.8 0.0 copy-done.3
  2.8 0.0 copy-done.4
  2.8 51.1 %shard_map.86 = (f32[125,1024]{1,0:T(8,128)S(1)}, f32[25,3072]{1,0:T(8,128)S(1)}) custom-call(f32[125,1024]{1,0:T(8,128)S(1)} %copy-done, f32[4,125,125]{2,1,0:T(8,128)S(1)} %copy.9.inverses, f32[125,150]{1,0:T(8,128)S(1)} %copy.10.lift, f32[4]{0:T(128)S(1)} %copy-done.4, s32[1,1024]{1,0:T(1,128)S(1)} %bitcast.1, s32[6,1024]{1,0:T(8,128)S(1)} %copy-done.1, ...), custom_call_target="tpu_custom_call" | custom-call | tf_op jit(solution)/shard_map/pallas_call | solution.py:435
  53.9 0.8 %copy.13 = f32[125,1024]{1,0:T(8,128)} copy(f32[125,1024]{1,0:T(8,128)S(1)} %get-tuple-element.4) | data formatting | bytes 1024000
  54.7 0.7 %copy.14 = f32[25,3072]{1,0:T(8,128)} copy(f32[25,3072]{1,0:T(8,128)S(1)} %get-tuple-element.5) | data formatting | bytes 614400
Async XLA Ops:
  0.6 2.1 %copy-start = (f32[125,1024]{1,0:T(8,128)S(1)}, f32[125,1024]{1,0:T(8,128)}, u32[]{:S(2)}) copy-start(f32[125,1024]{1,0:T(8,128)} %source.1) | copy-start | bytes 1536004
  1.7 1.1 %copy-start.1 = (s32[6,1024]{1,0:T(8,128)S(1)}, s32[6,1024]{1,0:T(8,128)}, u32[]{:S(2)}) copy-start(s32[6,1024]{1,0:T(8,128)} %face_slot.1) | copy-start | bytes 73732
  1.7 1.1 %copy-start.2 = (s32[1024]{0:T(1024)S(1)}, s32[1024]{0:T(1024)}, u32[]{:S(2)}) copy-start(s32[1024]{0:T(1024)} %param.11) | copy-start | bytes 12292
  1.7 1.1 %copy-start.3 = (s32[1,768]{1,0:T(1,128)S(1)}, s32[1,768]{1,0:T(1,128)}, u32[]{:S(2)}) copy-start(s32[1,768]{1,0:T(1,128)} %owner_map.1) | copy-start | bytes 9220
  1.7 1.1 %copy-start.4 = (f32[4]{0:T(128)S(1)}, f32[4]{0:T(128)}, u32[]{:S(2)}) copy-start(f32[4]{0:T(128)} %stab.1) | copy-start | bytes 52

commit v2 on v1

--- a/solution.py
+++ b/solution.py
@@ -185,7 +185,7 @@
         idx_f[s] = (idx - iota((16, ELEM), 0).astype(F32)).astype(BF)
         return carry
 
-    lax.fori_loop(0, SIDES, renumber, 0)
+    lax.fori_loop(0, SIDES, renumber, 0, unroll=True)
 
     def count(s, carry):
         idx = idx_f[s]
@@ -199,7 +199,7 @@
         counts[s] = dot_nt(ones, onehot[s])
         return carry
 
-    lax.fori_loop(0, SIDES, count, 0)
+    lax.fori_loop(0, SIDES, count, 0, unroll=True)
 
     inv_pad[...] = jnp.zeros_like(inv_pad)
     inv_pad[:, 0:NODES, 0:NODES] = inverses[...]
@@ -313,7 +313,7 @@
             partial[rows] += out
             return carry
 
-        lax.fori_loop(0, SIDES, add, 0)
+        lax.fori_loop(0, SIDES, add, 0, unroll=True)
 
     def fetch(name):
         first, last, main, left = GROUPS[name]
@@ -336,7 +336,7 @@
             x_left[s, 0:1] = acc_left + jnp.sum(yl[0] + yl[1], axis=0, keepdims=True)
             return carry
 
-        lax.fori_loop(0, SIDES, take, 0)
+        lax.fori_loop(0, SIDES, take, 0, unroll=True)
 
     def gathered():
         rows = [x_main[s] for s in range(SIDES)]

time: 55.9 us -> 53.1 us (0.950)
  Pallas kernels: 51.1 us -> 48.4 us
    pallas_call x1, Pallas kernels: 51.1 us -> 48.4 us  [shards(): pl.pallas_call(kernel, out_shape=(jax.ShapeDtypeStruct((NODES, ELEM), F32...]
where the time goes in v2:
time: 53.1 us; the launch traced here: 52.7 us
  Pallas kernels  48.4 us (91%)
  local copies, waits for them, and re-layouts  3.62 us (7%)
  between operations  0.72 us (1%)
    pallas_call x1, Pallas kernels, shards(): pl.pallas_call(kernel, out_shape=(jax.ShapeDtypeStruct((NODES, ELEM), F32...  48.4 us
    unnamed x14, local copies, waits for them, and re-layouts  3.62 us

profile of v2, /device:TPU:7, one launch (start us, length us, event | category | flops | bytes accessed | tf_op | source)
XLA Modules:
  0.0 52.7 jit_solution(11707566983915710544)
XLA Ops:
  0.6 0.0 copy-start
  0.6 1.1 %copy.10.lift = f32[125,150]{1,0:T(8,128)S(1)} copy(f32[125,150]{0,1:T(8,128)} %param.9) | data formatting | bytes 150000 | tf_op args[2]
  1.7 0.0 copy-start.1
  1.7 0.0 copy-start.2
  1.7 0.0 copy-start.3
  1.7 0.0 copy-start.4
  1.7 1.0 %copy.9.inverses = f32[4,125,125]{2,1,0:T(8,128)S(1)} copy(f32[4,125,125]{2,0,1:T(4,128)} %param.8) | data formatting | bytes 500000 | tf_op args[1]
  2.7 0.0 copy-done
  2.7 0.0 copy-done.1
  2.8 0.0 copy-done.2
  2.8 0.0 copy-done.3
  2.8 0.0 copy-done.4
  2.8 48.4 %shard_map.86 = (f32[125,1024]{1,0:T(8,128)S(1)}, f32[25,3072]{1,0:T(8,128)S(1)}) custom-call(f32[125,1024]{1,0:T(8,128)S(1)} %copy-done, f32[4,125,125]{2,1,0:T(8,128)S(1)} %copy.9.inverses, f32[125,150]{1,0:T(8,128)S(1)} %copy.10.lift, f32[4]{0:T(128)S(1)} %copy-done.4, s32[1,1024]{1,0:T(1,128)S(1)} %bitcast.1, s32[6,1024]{1,0:T(8,128)S(1)} %copy-done.1, ...), custom_call_target="tpu_custom_call" | custom-call | tf_op jit(solution)/shard_map/pallas_call | solution.py:435
  51.2 0.8 %copy.13 = f32[125,1024]{1,0:T(8,128)} copy(f32[125,1024]{1,0:T(8,128)S(1)} %get-tuple-element.4) | data formatting | bytes 1024000
  52.0 0.7 %copy.14 = f32[25,3072]{1,0:T(8,128)} copy(f32[25,3072]{1,0:T(8,128)S(1)} %get-tuple-element.5) | data formatting | bytes 614400
Async XLA Ops:
  0.6 2.1 %copy-start = (f32[125,1024]{1,0:T(8,128)S(1)}, f32[125,1024]{1,0:T(8,128)}, u32[]{:S(2)}) copy-start(f32[125,1024]{1,0:T(8,128)} %source.1) | copy-start | bytes 1536004
  1.7 1.1 %copy-start.1 = (s32[6,1024]{1,0:T(8,128)S(1)}, s32[6,1024]{1,0:T(8,128)}, u32[]{:S(2)}) copy-start(s32[6,1024]{1,0:T(8,128)} %face_slot.1) | copy-start | bytes 73732
  1.7 1.1 %copy-start.2 = (s32[1024]{0:T(1024)S(1)}, s32[1024]{0:T(1024)}, u32[]{:S(2)}) copy-start(s32[1024]{0:T(1024)} %param.11) | copy-start | bytes 12292
  1.7 1.1 %copy-start.3 = (s32[1,768]{1,0:T(1,128)S(1)}, s32[1,768]{1,0:T(1,128)}, u32[]{:S(2)}) copy-start(s32[1,768]{1,0:T(1,128)} %owner_map.1) | copy-start | bytes 9220
  1.7 1.1 %copy-start.4 = (f32[4]{0:T(128)S(1)}, f32[4]{0:T(128)}, u32[]{:S(2)}) copy-start(f32[4]{0:T(128)} %stab.1) | copy-start | bytes 52

commit v3 on v2

--- a/solution.py
+++ b/solution.py
@@ -70,29 +70,19 @@
 ):
     w, n = lax.axis_index("wide"), lax.axis_index("narrow")
     wide, narrow = lax.axis_size("wide"), lax.axis_size("narrow")
-    there = (w > 0, w < wide - 1, n > 0, n < narrow - 1)
-    neighbour = ((w - 1, n), (w + 1, n), (w, n - 1), (w, n + 1))
+    neighbour = (
+        (lax.rem(w + wide - 1, wide), n),
+        (lax.rem(w + 1, wide), n),
+        (w, lax.rem(n + narrow - 1, narrow)),
+        (w, lax.rem(n + 1, narrow)),
+    )
     barrier = pltpu.get_barrier_semaphore()
-    present = jnp.int32(0)
     for k in range(4):
-        present = present + there[k].astype(jnp.int32)
-
-        @pl.when(there[k])
-        def _():
-            pl.semaphore_signal(barrier, inc=1, device_id=neighbour[k], device_id_type=MESH)
-
-    pl.semaphore_wait(barrier, present)
+        pl.semaphore_signal(barrier, inc=1, device_id=neighbour[k], device_id_type=MESH)
+    pl.semaphore_wait(barrier, 4)
 
     def buffers(k):
         return (send_w, recv_w, k) if k < 2 else (send_n, recv_n, k - 2)
-
-    for k in range(4):
-        send, recv, side = buffers(k)
-
-        @pl.when(jnp.logical_not(there[k]))
-        def _():
-            for r in range(ROUNDS):
-                recv[r, side] = jnp.zeros(recv.shape[2:], F32)
 
     def copy(r, k):
         send, recv, side = buffers(k)
@@ -132,15 +122,11 @@
             send[r, side, 48:49] = values[ghost : ghost + 1, cols]
             send[r, side, 49:50] = values[shared : shared + 1, cols]
 
-            @pl.when(there[k])
-            def _():
-                copy(r, k).start()
+            copy(r, k).start()
 
     def collect(r, values):
         for k in range(4):
-            @pl.when(there[k])
-            def _():
-                arrival(r, k).wait_recv()
+            arrival(r, k).wait_recv()
 
         for k in range(4):
             send, recv, side = buffers(k)
@@ -423,9 +409,7 @@
 
     for r in range(ROUNDS):
         for k in range(4):
-            @pl.when(there[k])
-            def _():
-                copy(r, k).wait_send()
+            copy(r, k).wait_send()
 
 
 def shards(source, inverses, lift, stab, material, face_slot, owner_map):

time: 53.1 us -> 50.8 us (0.957)
  the two profiles are of different devices: /device:TPU:7 before, /device:TPU:0 now
where the time goes in v3:
time: 50.8 us; the launch traced here: 50.7 us
  Pallas kernels  46.4 us (91%)
  local copies, waits for them, and re-layouts  3.62 us (7%)
  between operations  0.72 us (1%)
    pallas_call x1, Pallas kernels, shards(): pl.pallas_call(kernel, out_shape=(jax.ShapeDtypeStruct((NODES, ELEM), F32...  46.4 us
    unnamed x14, local copies, waits for them, and re-layouts  3.62 us

profile of v3, /device:TPU:0, one launch (start us, length us, event | category | flops | bytes accessed | tf_op | source)
XLA Modules:
  0.0 50.7 jit_solution(15760521106598986265)
XLA Ops:
  0.6 0.0 copy-start
  0.6 1.1 %copy.10.lift = f32[125,150]{1,0:T(8,128)S(1)} copy(f32[125,150]{0,1:T(8,128)} %param.9) | data formatting | bytes 150000 | tf_op args[2]
  1.7 0.0 copy-start.1
  1.7 0.0 copy-start.2
  1.7 0.0 copy-start.3
  1.7 0.0 copy-start.4
  1.7 1.0 %copy.9.inverses = f32[4,125,125]{2,1,0:T(8,128)S(1)} copy(f32[4,125,125]{2,0,1:T(4,128)} %param.8) | data formatting | bytes 500000 | tf_op args[1]
  2.7 0.0 copy-done
  2.7 0.0 copy-done.1
  2.8 0.0 copy-done.2
  2.8 0.0 copy-done.3
  2.8 0.0 copy-done.4
  2.8 46.4 %shard_map.86 = (f32[125,1024]{1,0:T(8,128)S(1)}, f32[25,3072]{1,0:T(8,128)S(1)}) custom-call(f32[125,1024]{1,0:T(8,128)S(1)} %copy-done, f32[4,125,125]{2,1,0:T(8,128)S(1)} %copy.9.inverses, f32[125,150]{1,0:T(8,128)S(1)} %copy.10.lift, f32[4]{0:T(128)S(1)} %copy-done.4, s32[1,1024]{1,0:T(1,128)S(1)} %bitcast.1, s32[6,1024]{1,0:T(8,128)S(1)} %copy-done.1, ...), custom_call_target="tpu_custom_call" | custom-call | tf_op jit(solution)/shard_map/pallas_call | solution.py:419
  49.2 0.8 %copy.13 = f32[125,1024]{1,0:T(8,128)} copy(f32[125,1024]{1,0:T(8,128)S(1)} %get-tuple-element.4) | data formatting | bytes 1024000
  50.0 0.7 %copy.14 = f32[25,3072]{1,0:T(8,128)} copy(f32[25,3072]{1,0:T(8,128)S(1)} %get-tuple-element.5) | data formatting | bytes 614400
Async XLA Ops:
  0.6 2.1 %copy-start = (f32[125,1024]{1,0:T(8,128)S(1)}, f32[125,1024]{1,0:T(8,128)}, u32[]{:S(2)}) copy-start(f32[125,1024]{1,0:T(8,128)} %source.1) | copy-start | bytes 1536004
  1.7 1.1 %copy-start.1 = (s32[6,1024]{1,0:T(8,128)S(1)}, s32[6,1024]{1,0:T(8,128)}, u32[]{:S(2)}) copy-start(s32[6,1024]{1,0:T(8,128)} %face_slot.1) | copy-start | bytes 73732
  1.7 1.1 %copy-start.2 = (s32[1024]{0:T(1024)S(1)}, s32[1024]{0:T(1024)}, u32[]{:S(2)}) copy-start(s32[1024]{0:T(1024)} %param.11) | copy-start | bytes 12292
  1.7 1.1 %copy-start.3 = (s32[1,768]{1,0:T(1,128)S(1)}, s32[1,768]{1,0:T(1,128)}, u32[]{:S(2)}) copy-start(s32[1,768]{1,0:T(1,128)} %owner_map.1) | copy-start | bytes 9220
  1.7 1.1 %copy-start.4 = (f32[4]{0:T(128)S(1)}, f32[4]{0:T(128)}, u32[]{:S(2)}) copy-start(f32[4]{0:T(128)} %stab.1) | copy-start | bytes 52

commit v4 on v3

--- a/solution.py
+++ b/solution.py
@@ -70,11 +70,13 @@
 ):
     w, n = lax.axis_index("wide"), lax.axis_index("narrow")
     wide, narrow = lax.axis_size("wide"), lax.axis_size("narrow")
+    ends = (w == 0, w == wide - 1, n == 0, n == narrow - 1)
+    one = (w ^ 1, n ^ 1)
     neighbour = (
-        (lax.rem(w + wide - 1, wide), n),
-        (lax.rem(w + 1, wide), n),
-        (w, lax.rem(n + narrow - 1, narrow)),
-        (w, lax.rem(n + 1, narrow)),
+        (jnp.where(ends[0], w, w - 1), jnp.where(ends[0], one[1], n)),
+        (jnp.where(ends[1], w, w + 1), jnp.where(ends[1], one[1], n)),
+        (jnp.where(ends[2], one[0], w), jnp.where(ends[2], n, n - 1)),
+        (jnp.where(ends[3], one[0], w), jnp.where(ends[3], n, n + 1)),
     )
     barrier = pltpu.get_barrier_semaphore()
     for k in range(4):
@@ -88,9 +90,9 @@
         send, recv, side = buffers(k)
         return pltpu.make_async_remote_copy(
             src_ref=send.at[r, side],
-            dst_ref=recv.at[r, 1 - side],
+            dst_ref=recv.at[r, jnp.where(ends[k], side, 1 - side)],
             send_sem=send_sems.at[r, k],
-            recv_sem=recv_sems.at[r, k ^ 1],
+            recv_sem=recv_sems.at[r, jnp.where(ends[k], k, k ^ 1)],
             device_id=neighbour[k],
             device_id_type=MESH,
         )
@@ -188,9 +190,10 @@
     lax.fori_loop(0, SIDES, count, 0, unroll=True)
 
     inv_pad[...] = jnp.zeros_like(inv_pad)
-    inv_pad[:, 0:NODES, 0:NODES] = inverses[...]
+    for m in range(MATS):
+        inv_pad[m, 0:NODES, 0:NODES] = inverses[:, m, :]
     lift_pad[...] = jnp.zeros_like(lift_pad)
-    lift_pad[0:NODES, 0 : SIDES * FNODES] = lift[...]
+    lift_pad[0 : SIDES * FNODES, 0:NODES] = lift[...]
     src_pad[...] = jnp.zeros_like(src_pad)
     src_pad[0:NODES] = source[...]
     hi, lo = split(src_pad[...])
@@ -199,8 +202,7 @@
     side_p, node_p = trace_position(iota((TP, 256), 0))
     order = jnp.where(side_p < SIDES, 6 * node_p + side_p, -1)
     perm = (iota((TP, 256), 1) == order).astype(F32)
-    lift_t = dot_nt(perm, lift_pad[...], HIGH)
-    lift_p = dot_nt(lift_pad[...], perm, HIGH)
+    lift_t = dot(perm, lift_pad[...], HIGH)
     eye = iota((TP, TP), 0) == iota((TP, TP), 1)
     col = iota((TP, 192), 1)
     for i in range(1, 4):
@@ -209,9 +211,9 @@
     spread = jnp.zeros((TP, 192), F32)
     for m in range(MATS):
         inv = inv_pad[m]
-        wm = dot(inv, lift_p, HIGH)
+        wm = dot_nt(inv, lift_t, HIGH)
         wt = dot(lift_t, inv, HIGH)
-        am = dot(wt, lift_p, HIGH)
+        am = dot_nt(wt, lift_t, HIGH)
         diagonal = jnp.abs(jnp.sum(jnp.where(eye, am, 0.0), axis=1, keepdims=True)) + stab[m]
         spread = spread + jnp.where(col == 8 * side_c + m, diagonal, 0.0)
         am = am + jnp.where(eye, stab[m], 0.0)
@@ -432,7 +434,7 @@
             v((SIDES, 16, ELEM), BF),
             v((SIDES, 8 * BLOCKS, 256), F32),
             v((MATS, NP, NP), F32),
-            v((NP, 256), F32),
+            v((256, NP), F32),
             v((NP, ELEM), F32),
             v((3 * NP, ELEM), BF),
             v((MATS * (TP + NP), 3 * NP), BF),
@@ -461,7 +463,15 @@
         compiler_params=pltpu.CompilerParams(
             collective_id=0, has_side_effects=True, vmem_limit_bytes=48 * 2**20
         ),
-    )(source, inverses, lift, stab, material.reshape(1, ELEM), face_slot, owner_map)
+    )(
+        source,
+        inverses.transpose(1, 0, 2),
+        lift.T,
+        stab,
+        material.reshape(1, ELEM),
+        face_slot,
+        owner_map,
+    )
 
 
 def solution(mesh):

time: 50.8 us -> 49 us (0.965)
  the two profiles are of different devices: /device:TPU:0 before, /device:TPU:7 now
where the time goes in v4:
time: 49 us; the launch traced here: 48.6 us
  Pallas kernels  41.4 us (84%)
  local copies, waits for them, and re-layouts  6.53 us (13%)
  between operations  0.66 us (1%)
    pallas_call x1, Pallas kernels, shards(): pl.pallas_call(kernel, out_shape=(jax.ShapeDtypeStruct((NODES, ELEM), F32...  41.4 us
    unnamed x16, local copies, waits for them, and re-layouts  6.53 us

profile of v4, /device:TPU:7, one launch (start us, length us, event | category | flops | bytes accessed | tf_op | source)
XLA Modules:
  0.0 48.6 jit_solution(5589125039521768417)
XLA Ops:
  0.6 0.0 copy-start.4
  0.6 0.0 copy-start.6
  0.7 0.7 %copy-done.4 = s32[1024]{0:T(1024)S(1)} copy-done((s32[1024]{0:T(1024)S(1)}, s32[1024]{0:T(1024)}, u32[]{:S(2)}) %copy-start.4) | copy-done | bytes 4120
  1.3 0.0 copy-done.6
  1.3 0.0 copy-start
  1.3 1.0 %copy-done = f32[125,1024]{1,0:T(8,128)S(1)} copy-done((f32[125,1024]{1,0:T(8,128)S(1)}, f32[125,1024]{1,0:T(8,128)}, u32[]{:S(2)}) %copy-start) | copy-done | bytes 512024
  2.4 0.0 copy-start.1
  2.4 0.9 %copy-done.1 = f32[4,125,125]{2,0,1:T(4,128)S(1)} copy-done((f32[4,125,125]{2,0,1:T(4,128)S(1)}, f32[4,125,125]{2,0,1:T(4,128)}, u32[]{:S(2)}) %copy-start.1) | copy-done | bytes 250024
  3.3 0.0 copy-start.2
  3.3 0.9 %copy-done.2 = f32[125,150]{0,1:T(8,128)S(1)} copy-done((f32[125,150]{0,1:T(8,128)S(1)}, f32[125,150]{0,1:T(8,128)}, u32[]{:S(2)}) %copy-start.2) | copy-done | bytes 75024
  4.2 0.0 copy-start.3
  4.2 0.8 %copy-done.3 = s32[6,1024]{1,0:T(8,128)S(1)} copy-done((s32[6,1024]{1,0:T(8,128)S(1)}, s32[6,1024]{1,0:T(8,128)}, u32[]{:S(2)}) %copy-start.3) | copy-done | bytes 24600
  5.0 0.0 copy-start.5
  5.0 0.7 %copy-done.5 = s32[1,768]{1,0:T(1,128)S(1)} copy-done((s32[1,768]{1,0:T(1,128)S(1)}, s32[1,768]{1,0:T(1,128)}, u32[]{:S(2)}) %copy-start.5) | copy-done | bytes 3096
  5.6 41.4 %shard_map.86 = (f32[125,1024]{1,0:T(8,128)S(1)}, f32[25,3072]{1,0:T(8,128)S(1)}) custom-call(f32[125,1024]{1,0:T(8,128)S(1)} %copy-done, f32[125,4,125]{2,1,0:T(4,128)S(1)} %bitcast.3, f32[150,125]{1,0:T(8,128)S(1)} %bitcast.4, f32[4]{0:T(128)S(1)} %copy-done.6, s32[1,1024]{1,0:T(1,128)S(1)} %bitcast.5, s32[6,1024]{1,0:T(8,128)S(1)} %copy-done.3, ...), custom_call_target="tpu_custom_call" | custom-call | tf_op jit(solution)/shard_map/pallas_call | solution.py:421
  47.1 0.8 %copy.11 = f32[125,1024]{1,0:T(8,128)} copy(f32[125,1024]{1,0:T(8,128)S(1)} %get-tuple-element.4) | data formatting | bytes 1024000
  47.9 0.7 %copy.12 = f32[25,3072]{1,0:T(8,128)} copy(f32[25,3072]{1,0:T(8,128)S(1)} %get-tuple-element.5) | data formatting | bytes 614400
Async XLA Ops:
  0.6 0.7 %copy-start.4 = (s32[1024]{0:T(1024)S(1)}, s32[1024]{0:T(1024)}, u32[]{:S(2)}) copy-start(s32[1024]{0:T(1024)} %param.11) | copy-start | bytes 12292
  0.6 0.7 %copy-start.6 = (f32[4]{0:T(128)S(1)}, f32[4]{0:T(128)}, u32[]{:S(2)}) copy-start(f32[4]{0:T(128)} %stab.1) | copy-start | bytes 52
  1.3 1.0 %copy-start = (f32[125,1024]{1,0:T(8,128)S(1)}, f32[125,1024]{1,0:T(8,128)}, u32[]{:S(2)}) copy-start(f32[125,1024]{1,0:T(8,128)} %source.1) | copy-start | bytes 1536004
  2.4 0.9 %copy-start.1 = (f32[4,125,125]{2,0,1:T(4,128)S(1)}, f32[4,125,125]{2,0,1:T(4,128)}, u32[]{:S(2)}) copy-start(f32[4,125,125]{2,0,1:T(4,128)} %param.8) | copy-start | bytes 750004
  3.3 0.9 %copy-start.2 = (f32[125,150]{0,1:T(8,128)S(1)}, f32[125,150]{0,1:T(8,128)}, u32[]{:S(2)}) copy-start(f32[125,150]{0,1:T(8,128)} %param.9) | copy-start | bytes 225004
  4.2 0.8 %copy-start.3 = (s32[6,1024]{1,0:T(8,128)S(1)}, s32[6,1024]{1,0:T(8,128)}, u32[]{:S(2)}) copy-start(s32[6,1024]{1,0:T(8,128)} %face_slot.1) | copy-start | bytes 73732
  5.0 0.7 %copy-start.5 = (s32[1,768]{1,0:T(1,128)S(1)}, s32[1,768]{1,0:T(1,128)}, u32[]{:S(2)}) copy-start(s32[1,768]{1,0:T(1,128)} %owner_map.1) | copy-start | bytes 9220

commit v5 on v4

--- a/solution.py
+++ b/solution.py
@@ -8,7 +8,8 @@
 from jax.sharding import PartitionSpec as P
 
 MESH = pl.DeviceIdType.MESH
-F32, BF = jnp.float32, jnp.bfloat16
+F32, BF, F8 = jnp.float32, jnp.bfloat16, jnp.float8_e4m3fn
+FULL = 3500.0
 HIGH = lax.Precision.HIGHEST
 DAMPING = 0.6
 SWEEPS = 3
@@ -22,11 +23,12 @@
 NP = 128
 
 OWN_BLOCKS, BLOCKS = 12, 18
-OWN_MAIN, OWN_LEFT, OUT_MAIN, OUT_LEFT, ROWS = 0, 288, 304, 448, 464
+OWN_MAIN, OWN_LEFT, OUT_MAIN, OUT_LEFT, ROWS = 0, 288, 320, 464, 480
 GROUPS = {
-    "own": (0, 12, OWN_MAIN, OWN_LEFT),
-    "out": (12, 18, OUT_MAIN, OUT_LEFT),
+    "own": (0, 12, OWN_MAIN, OWN_LEFT, slice(0, 320)),
+    "out": (12, 18, OUT_MAIN, OUT_LEFT, slice(320, 480)),
 }
+WEIGHTS = (16.0, 1.0, 0.0625)
 SENT = 56
 ROUNDS = 2 + SWEEPS - 1
 
@@ -44,6 +46,20 @@
 def split(x):
     hi = x.astype(BF)
     return hi, (x - hi.astype(F32)).astype(BF)
+
+
+def split8(v):
+    a = (v * 0.0625).astype(F8)
+    r = v - 16.0 * a.astype(F32)
+    b = r.astype(F8)
+    c = ((r - b.astype(F32)) * 16.0).astype(F8)
+    return a, b, c
+
+
+def scaling(x):
+    m = jnp.max(jnp.max(jnp.abs(x), axis=0, keepdims=True), axis=1, keepdims=True)
+    m = jnp.maximum(m, 1e-30)
+    return FULL / m, m * (1.0 / FULL)
 
 
 def iota(shape, dim):
@@ -60,14 +76,31 @@
 
 
 def kernel(
+    source_hbm, inverses_hbm, lift_hbm, stab_hbm, material_hbm, face_slot_hbm, owner_map_hbm,
+    potential, trace_own,
     source, inverses, lift, stab, material, face_slot, owner_map,
-    potential, trace_own,
     onehot, onehot_out, blk_f, blk_d, idx_f, counts,
     inv_pad, lift_pad, src_pad, src3, left3, a3, w3,
-    rhs_terms, x_main, x_left, x3, t_hi, t_lo, l_hi, l_lo,
-    partial, total, table, table2, scale,
-    send_w, recv_w, send_n, recv_n, send_sems, recv_sems,
+    rhs_terms, terms, x_main, x_left, x3, t_parts, l_parts,
+    partial, total, table, scale,
+    send_w, recv_w, send_n, recv_n, send_sems, recv_sems, in_sems,
 ):
+    loads = [
+        pltpu.make_async_copy(src, dst, in_sems.at[i])
+        for i, (src, dst) in enumerate(
+            (
+                (face_slot_hbm, face_slot),
+                (owner_map_hbm, owner_map),
+                (material_hbm, material),
+                (inverses_hbm, inverses),
+                (lift_hbm, lift),
+                (stab_hbm, stab),
+                (source_hbm, source),
+            )
+        )
+    ]
+    for load in loads:
+        load.start()
     w, n = lax.axis_index("wide"), lax.axis_index("narrow")
     wide, narrow = lax.axis_size("wide"), lax.axis_size("narrow")
     ends = (w == 0, w == wide - 1, n == 0, n == narrow - 1)
@@ -140,6 +173,8 @@
             values[shared : shared + 1, cols] += recv[r, side, 48:49]
             values[ghost : ghost + 1, cols] += recv[r, side, 49:50]
 
+    for load in loads[:3]:
+        load.wait()
     owners = owner_map[...]
     own_blk, own_col = owners >> 8, owners & 255
     place = iota((1, GHOSTS), 1) + 1
@@ -165,7 +200,9 @@
             jnp.where(hit, 256.0 * found[0:16] + found[16:32], 0.0), axis=0, keepdims=True
         ).astype(jnp.int32)
         v = jnp.where(spot > 0, OWNED + GHOSTS - 1 + spot, v)
-        onehot[s] = (iota((256, ELEM), 0) == (v & 255)).astype(F32).astype(BF)
+        met = iota((256, ELEM), 0) == (v & 255)
+        for p, weight in enumerate(WEIGHTS):
+            onehot[p, s] = jnp.where(met, weight, 0.0).astype(F8)
         blk = (v >> 8).astype(F32)
         blk_f[s] = jnp.broadcast_to(blk, (8, ELEM))
         blk_d[s] = (blk - (iota((48, ELEM), 0) >= 24).astype(F32)).astype(BF)
@@ -180,15 +217,17 @@
         ones = jnp.concatenate(
             [
                 jnp.where(idx == BF(16 * t), BF(1), BF(0))
-                for t in range(8 * BLOCKS // 16)
+                for t in range(10)
             ],
             axis=0,
         )
-        counts[s] = dot_nt(ones, onehot[s])
+        counts[s] = dot_nt(ones.astype(F8), onehot[1, s])
         return carry
 
     lax.fori_loop(0, SIDES, count, 0, unroll=True)
 
+    for load in loads[3:]:
+        load.wait()
     inv_pad[...] = jnp.zeros_like(inv_pad)
     for m in range(MATS):
         inv_pad[m, 0:NODES, 0:NODES] = inverses[:, m, :]
@@ -214,9 +253,9 @@
         wm = dot_nt(inv, lift_t, HIGH)
         wt = dot(lift_t, inv, HIGH)
         am = dot_nt(wt, lift_t, HIGH)
-        diagonal = jnp.abs(jnp.sum(jnp.where(eye, am, 0.0), axis=1, keepdims=True)) + stab[m]
+        diagonal = jnp.abs(jnp.sum(jnp.where(eye, am, 0.0), axis=1, keepdims=True)) + stab[0:1, m : m + 1]
         spread = spread + jnp.where(col == 8 * side_c + m, diagonal, 0.0)
-        am = am + jnp.where(eye, stab[m], 0.0)
+        am = am + jnp.where(eye, stab[0:1, m : m + 1], 0.0)
         hi, lo = split(am)
         a3[TP * m : TP * (m + 1)] = jnp.concatenate([hi, hi, lo], axis=1)
         hi, lo = split(wm)
@@ -236,7 +275,7 @@
     sdiag = jnp.where(iota((32, 192), 1) < 96, hi, sdiag - hi).astype(BF)
 
     def diag_block(a):
-        _, _, main, left = GROUPS["own" if a < OWN_BLOCKS else "out"]
+        _, _, main, left, _ = GROUPS["own" if a < OWN_BLOCKS else "out"]
         b = a if a < OWN_BLOCKS else a - OWN_BLOCKS
         met = jnp.concatenate([counts[s, 8 * a : 8 * a + 8] for s in range(SIDES)], axis=0)
         hi, lo = split(met)
@@ -265,66 +304,59 @@
         rhs_terms[:, e] = pick(y[0 : MATS * TP], TP, e)
         potential[:, e] = pick(y[MATS * TP :], NP, e)[0:NODES]
 
-    def store_terms(terms, e):
+    def store_terms(source_terms):
+        up, down = scaling(source_terms[...])
         for s in range(SIDES):
-            t = terms[24 * s : 24 * s + 24]
-            hi, lo = split(jnp.concatenate([t, t], axis=0))
-            t_hi[s, :, e], t_lo[s, :, e] = hi, lo
-            t = jnp.broadcast_to(terms[144 + s : 145 + s], (16, terms.shape[1]))
-            hi, lo = split(t)
-            l_hi[s, :, e], l_lo[s, :, e] = hi, lo
-
-    for c in range(ELEM // CHUNK):
-        e = slice(c * CHUNK, (c + 1) * CHUNK)
-        store_terms(rhs_terms[:, e], e)
+            t = source_terms[24 * s : 24 * s + 24] * up
+            l = jnp.broadcast_to(source_terms[144 + s : 145 + s] * up, (16, ELEM))
+            for p, part in enumerate(split8(jnp.concatenate([t, t], axis=0))):
+                t_parts[p, s] = part.astype(BF)
+            for p, part in enumerate(split8(l)):
+                l_parts[p, s] = part.astype(BF)
+        return down
+
+    terms_down = store_terms(rhs_terms)
 
     def row_ids(first, last, dtype):
         r = iota((16, ELEM), 0)
         return jnp.where(r < last - first, r + first, -1).astype(F32).astype(dtype)
 
-    def assemble(name):
-        first, last, main, left = GROUPS[name]
-        rows = slice(main, left + 16)
-        partial[rows] = jnp.zeros((left + 16 - main, 256), F32)
-
-        def add(s, carry):
+    def assemble(name, down):
+        first, last, _, _, rows = GROUPS[name]
+        out = None
+        for s in range(SIDES):
             hit = row_ids(first, last, BF) == blk_d[s, 0:16]
             hits = [blk_d[s] == BF(a) for a in range(first, last, 2)]
-            out = None
-            for t, l in ((t_hi, l_hi), (t_lo, l_lo)):
-                tv = t[s]
-                z = jnp.concatenate(
-                    [jnp.where(h, tv, BF(0)) for h in hits] + [jnp.where(hit, l[s], BF(0))], axis=0
-                )
-                d = dot_nt(z, onehot[s])
+            for p in range(3):
+                t = t_parts[p, s]
+                z = [jnp.where(h, t, BF(0)) for h in hits]
+                z.append(jnp.where(hit, l_parts[p, s], BF(0)))
+                if name == "own":
+                    z.append(jnp.zeros((16, ELEM), BF))
+                d = dot_nt(jnp.concatenate(z, axis=0).astype(F8), onehot[p, s])
                 out = d if out is None else out + d
-            partial[rows] += out
-            return carry
-
-        lax.fori_loop(0, SIDES, add, 0, unroll=True)
-
-    def fetch(name):
-        first, last, main, left = GROUPS[name]
-
-        def take(s, carry):
-            y = dot(table[main : left + 16], onehot[s]) + dot(table2[main : left + 16], onehot[s])
+        partial[rows] = out * down
+
+    def fetch(name, down):
+        first, last, main, left, rows = GROUPS[name]
+        for s in range(SIDES):
+            y = dot(table[0, rows], onehot[0, s])
+            for p in (1, 2):
+                y = y + dot(table[p, rows], onehot[p, s])
             blk = blk_f[s]
-            if name == "own":
-                acc = jnp.zeros((3, 8, ELEM), F32)
-                acc_left = jnp.zeros((1, ELEM), F32)
-            else:
-                acc = x_main[s].reshape(3, 8, ELEM)
-                acc_left = x_left[s, 0:1]
+            acc = jnp.zeros((3, 8, ELEM), F32)
             for a in range(first, last):
                 ya = y[24 * (a - first) : 24 * (a - first) + 24].reshape(3, 8, ELEM)
                 acc = jnp.where((blk == F32(a))[None], ya, acc)
-            x_main[s] = acc.reshape(24, ELEM)
+            acc = acc.reshape(24, ELEM) * down
             hit = row_ids(first, last, F32).reshape(2, 8, ELEM) == blk[None]
-            yl = jnp.where(hit, y[left - main :].reshape(2, 8, ELEM), 0.0)
-            x_left[s, 0:1] = acc_left + jnp.sum(yl[0] + yl[1], axis=0, keepdims=True)
-            return carry
-
-        lax.fori_loop(0, SIDES, take, 0, unroll=True)
+            yl = jnp.where(hit, y[left - main : left - main + 16].reshape(2, 8, ELEM), 0.0)
+            acc_left = jnp.sum(yl[0] + yl[1], axis=0, keepdims=True) * down
+            if name == "out":
+                acc = acc + x_main[s]
+                acc_left = acc_left + x_left[s, 0:1]
+            x_main[s] = acc
+            x_left[s, 0:1] = acc_left
 
     def gathered():
         rows = [x_main[s] for s in range(SIDES)]
@@ -333,52 +365,47 @@
         hi, lo = split(x)
         x3[0:TP], x3[TP : 2 * TP], x3[2 * TP :] = hi, lo, hi
 
-    def table_rows(name):
-        _, _, main, left = GROUPS[name]
-        return slice(main, left + 16)
-
     def update(name, first):
-        rows = table_rows(name)
+        rows = GROUPS[name][4]
         step = scale[rows] * partial[rows]
         x = step if first else total[rows] + step
         total[rows] = x
-        hi, lo = split(x)
-        table[rows], table2[rows] = hi, lo
-
-    assemble("out")
+        up, down = scaling(x)
+        for p, part in enumerate(split8(x * up)):
+            table[p, rows] = part
+        return down
+
+    assemble("out", terms_down)
     post(1, partial)
     for a in range(OWN_BLOCKS):
         diag_block(a)
-    assemble("own")
+    assemble("own", terms_down)
 
     def invert(name):
-        rows = table_rows(name)
+        rows = GROUPS[name][4]
         d = scale[rows]
         scale[rows] = jnp.where(d == 0.0, 0.0, DAMPING / jnp.where(d == 0.0, 1.0, d))
 
     invert("own")
-    update("own", True)
-    fetch("own")
+    fetch("own", update("own", True))
     collect(0, scale)
     collect(1, partial)
     invert("out")
-    update("out", True)
-    fetch("out")
+    fetch("out", update("out", True))
 
     for sweep in range(SWEEPS - 1):
         gathered()
         for c in range(ELEM // CHUNK):
             e = slice(c * CHUNK, (c + 1) * CHUNK)
             y = pick(dot(a3[...], x3[:, e]), TP, e)
-            store_terms(rhs_terms[:, e] - y, e)
-        assemble("out")
+            terms[:, e] = rhs_terms[:, e] - y
+        terms_down = store_terms(terms)
+        assemble("out", terms_down)
         post(2 + sweep, partial)
-        assemble("own")
-        update("own", False)
-        fetch("own")
+        assemble("own", terms_down)
+        fetch("own", update("own", False))
         collect(2 + sweep, partial)
-        update("out", False)
-        fetch("out")
+        fetch("out", update("out", False))
 
     rows = slice(OWN_MAIN, OWN_LEFT + 16)
     back = jnp.zeros((304, 256), F32)
@@ -416,7 +443,7 @@
 
 def shards(source, inverses, lift, stab, material, face_slot, owner_map):
     vmem = pl.BlockSpec(memory_space=pltpu.VMEM)
-    smem = pl.BlockSpec(memory_space=pltpu.SMEM)
+    hbm = pl.BlockSpec(memory_space=pltpu.HBM)
     v = pltpu.VMEM
     return pl.pallas_call(
         kernel,
@@ -424,15 +451,22 @@
             jax.ShapeDtypeStruct((NODES, ELEM), F32),
             jax.ShapeDtypeStruct((FNODES, OWNED), F32),
         ),
-        in_specs=[vmem, vmem, vmem, smem, vmem, vmem, vmem],
+        in_specs=[hbm] * 7,
         out_specs=(vmem, vmem),
         scratch_shapes=[
-            v((SIDES, 256, ELEM), BF),
+            v((NODES, ELEM), F32),
+            v((NODES, MATS, NODES), F32),
+            v((SIDES * FNODES, NODES), F32),
+            v((1, MATS), F32),
+            v((1, ELEM), jnp.int32),
+            v((SIDES, ELEM), jnp.int32),
+            v((1, GHOSTS), jnp.int32),
+            v((3, SIDES, 256, ELEM), F8),
             v((256, GHOSTS), BF),
             v((SIDES, 8, ELEM), F32),
             v((SIDES, 48, ELEM), BF),
             v((SIDES, 16, ELEM), BF),
-            v((SIDES, 8 * BLOCKS, 256), F32),
+            v((SIDES, 160, 256), F32),
             v((MATS, NP, NP), F32),
             v((256, NP), F32),
             v((NP, ELEM), F32),
@@ -441,17 +475,15 @@
             v((MATS * TP, 3 * TP), BF),
             v((MATS * NP, 3 * TP), BF),
             v((TP, ELEM), F32),
+            v((TP, ELEM), F32),
             v((SIDES, 24, ELEM), F32),
             v((SIDES, 8, ELEM), F32),
             v((3 * TP, ELEM), BF),
-            v((SIDES, 48, ELEM), BF),
-            v((SIDES, 48, ELEM), BF),
-            v((SIDES, 16, ELEM), BF),
-            v((SIDES, 16, ELEM), BF),
+            v((3, SIDES, 48, ELEM), BF),
+            v((3, SIDES, 16, ELEM), BF),
             v((ROWS, 256), F32),
             v((ROWS, 256), F32),
-            v((ROWS, 256), BF),
-            v((ROWS, 256), BF),
+            v((3, ROWS, 256), F8),
             v((ROWS, 256), F32),
             v((ROUNDS, 2, SENT, CAP_W), F32),
             v((ROUNDS, 2, SENT, CAP_W), F32),
@@ -459,15 +491,16 @@
             v((ROUNDS, 2, SENT, CAP_N), F32),
             pltpu.SemaphoreType.DMA((ROUNDS, 4)),
             pltpu.SemaphoreType.DMA((ROUNDS, 4)),
+            pltpu.SemaphoreType.DMA((7,)),
         ],
         compiler_params=pltpu.CompilerParams(
-            collective_id=0, has_side_effects=True, vmem_limit_bytes=48 * 2**20
+            collective_id=0, has_side_effects=True, vmem_limit_bytes=63 * 2**20
         ),
     )(
         source,
         inverses.transpose(1, 0, 2),
         lift.T,
-        stab,
+        stab.reshape(1, MATS),
         material.reshape(1, ELEM),
         face_slot,
         owner_map,

time: 49 us -> 43.7 us (0.89)
  local copies, waits for them, and re-layouts: 6.53 us -> 2.68 us
  Pallas kernels: 41.4 us -> 40.2 us
    unnamed x16 -> x4, local copies, waits for them, and re-layouts: 6.53 us -> 2.68 us
    pallas_call x1, Pallas kernels: 41.4 us -> 40.2 us  [shards(): pl.pallas_call(kernel, out_shape=(jax.ShapeDtypeStruct((NODES, ELEM), F32...]
where the time goes in v5:
time: 43.7 us; the launch traced here: 43.5 us
  Pallas kernels  40.2 us (92%)
  local copies, waits for them, and re-layouts  2.68 us (6%)
  between operations  0.65 us (1%)
    pallas_call x1, Pallas kernels, shards(): pl.pallas_call(kernel, out_shape=(jax.ShapeDtypeStruct((NODES, ELEM), F32...  40.2 us
    unnamed x4, local copies, waits for them, and re-layouts  2.68 us

profile of v5, /device:TPU:7, one launch (start us, length us, event | category | flops | bytes accessed | tf_op | source)
XLA Modules:
  0.0 43.5 jit_solution(685755934727784719)
XLA Ops:
  0.6 40.2 %shard_map.86 = (f32[125,1024]{1,0:T(8,128)}, f32[25,3072]{1,0:T(8,128)}) custom-call(f32[125,1024]{1,0:T(8,128)} %source_hbm.1, f32[125,4,125]{2,1,0:T(4,128)} %bitcast.4, f32[150,125]{1,0:T(8,128)} %bitcast.5, f32[1,4]{1,0:T(1,128)} %bitcast.7, s32[1,1024]{1,0:T(1,128)} %bitcast.6, s32[6,1024]{1,0:T(8,128)} %face_slot_hbm.1, s32[1,768]{1,0:T(1,128)} %owner_map_hbm.1), custom_call_target="tpu_custom_call" | custom-call | tf_op jit(solution)/shard_map/pallas_call | solution.py:448
  40.8 0.0 copy-start
  40.9 1.9 %copy.11 = f32[125,1024]{1,0:T(8,128)} copy(f32[125,1024]{1,0:T(8,128)} %get-tuple-element.4) | data formatting | bytes 1024000
  42.8 0.0 copy-done
  42.8 0.7 %copy.12 = f32[25,3072]{1,0:T(8,128)} copy(f32[25,3072]{1,0:T(8,128)S(1)} %copy-done) | data formatting | bytes 614400
Async XLA Ops:
  40.8 1.9 %copy-start = (f32[25,3072]{1,0:T(8,128)S(1)}, f32[25,3072]{1,0:T(8,128)}, u32[]{:S(2)}) copy-start(f32[25,3072]{1,0:T(8,128)} %get-tuple-element.5) | copy-start | bytes 921604

commit v6 on v5

--- a/solution.py
+++ b/solution.py
@@ -10,7 +10,6 @@
 MESH = pl.DeviceIdType.MESH
 F32, BF, F8 = jnp.float32, jnp.bfloat16, jnp.float8_e4m3fn
 FULL = 3500.0
-HIGH = lax.Precision.HIGHEST
 DAMPING = 0.6
 SWEEPS = 3
 
@@ -56,8 +55,15 @@
     return a, b, c
 
 
-def scaling(x):
-    m = jnp.max(jnp.max(jnp.abs(x), axis=0, keepdims=True), axis=1, keepdims=True)
+def dot3(a, b, product):
+    return product(a[0], b[0]) + (product(a[0], b[1]) + product(a[1], b[0]))
+
+
+def largest(x):
+    return jnp.max(jnp.max(jnp.abs(x), axis=0, keepdims=True), axis=1, keepdims=True)
+
+
+def factors(m):
     m = jnp.maximum(m, 1e-30)
     return FULL / m, m * (1.0 / FULL)
 
@@ -81,7 +87,7 @@
     source, inverses, lift, stab, material, face_slot, owner_map,
     onehot, onehot_out, blk_f, blk_d, idx_f, counts,
     inv_pad, lift_pad, src_pad, src3, left3, a3, w3,
-    rhs_terms, terms, x_main, x_left, x3, t_parts, l_parts,
+    rhs_terms, x_main, x_left, x3, t_parts, l_parts,
     partial, total, table, scale,
     send_w, recv_w, send_n, recv_n, send_sems, recv_sems, in_sems,
 ):
@@ -114,7 +120,6 @@
     barrier = pltpu.get_barrier_semaphore()
     for k in range(4):
         pl.semaphore_signal(barrier, inc=1, device_id=neighbour[k], device_id_type=MESH)
-    pl.semaphore_wait(barrier, 4)
 
     def buffers(k):
         return (send_w, recv_w, k) if k < 2 else (send_n, recv_n, k - 2)
@@ -192,17 +197,17 @@
 
     def renumber(s, carry):
         v = face_slot[pl.ds(s, 1), :]
-        col = jnp.broadcast_to(v & 255, (256, ELEM))
-        first = (iota((256, ELEM), 0) == col).astype(F32).astype(BF)
+        row = iota((256, ELEM), 0).astype(F32).astype(BF)
+        first = jnp.where(row == (v & 255).astype(F32).astype(BF), BF(1), BF(0))
         found = dot(place_table, first)
         hit = iota((16, ELEM), 0) == (v >> 8)
         spot = jnp.sum(
             jnp.where(hit, 256.0 * found[0:16] + found[16:32], 0.0), axis=0, keepdims=True
         ).astype(jnp.int32)
         v = jnp.where(spot > 0, OWNED + GHOSTS - 1 + spot, v)
-        met = iota((256, ELEM), 0) == (v & 255)
+        met = row == (v & 255).astype(F32).astype(BF)
         for p, weight in enumerate(WEIGHTS):
-            onehot[p, s] = jnp.where(met, weight, 0.0).astype(F8)
+            onehot[p, s] = jnp.where(met, BF(weight), BF(0)).astype(F8)
         blk = (v >> 8).astype(F32)
         blk_f[s] = jnp.broadcast_to(blk, (8, ELEM))
         blk_d[s] = (blk - (iota((48, ELEM), 0) >= 24).astype(F32)).astype(BF)
@@ -240,8 +245,11 @@
 
     side_p, node_p = trace_position(iota((TP, 256), 0))
     order = jnp.where(side_p < SIDES, 6 * node_p + side_p, -1)
-    perm = (iota((TP, 256), 1) == order).astype(F32)
-    lift_t = dot(perm, lift_pad[...], HIGH)
+    perm = (iota((TP, 256), 1) == order).astype(F32).astype(BF)
+    hi, lo = split(lift_pad[...])
+    last = (lift_pad[...] - hi.astype(F32) - lo.astype(F32)).astype(BF)
+    lift_t = split(dot(perm, hi) + dot(perm, lo) + dot(perm, last))
+    row_sum = jnp.zeros((TP, 1), F32)
     eye = iota((TP, TP), 0) == iota((TP, TP), 1)
     col = iota((TP, 192), 1)
     for i in range(1, 4):
@@ -249,21 +257,19 @@
     side_c, _ = trace_position(iota((TP, 192), 0))
     spread = jnp.zeros((TP, 192), F32)
     for m in range(MATS):
-        inv = inv_pad[m]
-        wm = dot_nt(inv, lift_t, HIGH)
-        wt = dot(lift_t, inv, HIGH)
-        am = dot_nt(wt, lift_t, HIGH)
+        inv = split(inv_pad[m])
+        wt = dot3(lift_t, inv, dot)
+        am = dot3(split(wt), lift_t, dot_nt)
         diagonal = jnp.abs(jnp.sum(jnp.where(eye, am, 0.0), axis=1, keepdims=True)) + stab[0:1, m : m + 1]
         spread = spread + jnp.where(col == 8 * side_c + m, diagonal, 0.0)
         am = am + jnp.where(eye, stab[0:1, m : m + 1], 0.0)
         hi, lo = split(am)
         a3[TP * m : TP * (m + 1)] = jnp.concatenate([hi, hi, lo], axis=1)
-        hi, lo = split(wm)
-        w3[NP * m : NP * (m + 1)] = jnp.concatenate([hi, hi, lo], axis=1)
+        row_sum = jnp.maximum(row_sum, jnp.sum(jnp.abs(am), axis=1, keepdims=True))
         hi, lo = split(wt)
         r = slice(TP * m, TP * (m + 1))
         left3[r, 0:NP], left3[r, NP : 2 * NP], left3[r, 2 * NP :] = hi, hi, lo
-        hi, lo = split(inv)
+        hi, lo = inv
         r = slice(MATS * TP + NP * m, MATS * TP + NP * (m + 1))
         left3[r, 0:NP], left3[r, NP : 2 * NP], left3[r, 2 * NP :] = hi, hi, lo
     sdiag = jnp.zeros((24, 192), F32)
@@ -283,11 +289,6 @@
         scale[main + 24 * b : main + 24 * b + 24] = d[0:24]
         scale[left + b : left + b + 1] = d[24:25]
 
-    scale[...] = jnp.zeros_like(scale)
-    for a in range(OWN_BLOCKS, BLOCKS):
-        diag_block(a)
-    post(0, scale)
-
     mat = material[...]
 
     def pick(y, width, e):
@@ -300,22 +301,24 @@
     CHUNK = 512
     for c in range(ELEM // CHUNK):
         e = slice(c * CHUNK, (c + 1) * CHUNK)
-        y = dot(left3[...], src3[:, e])
-        rhs_terms[:, e] = pick(y[0 : MATS * TP], TP, e)
-        potential[:, e] = pick(y[MATS * TP :], NP, e)[0:NODES]
-
-    def store_terms(source_terms):
-        up, down = scaling(source_terms[...])
+        rhs_terms[:, e] = pick(dot(left3[0 : MATS * TP], src3[:, e]), TP, e)
+
+    def store_terms(values, e, up):
+        width = values.shape[1]
         for s in range(SIDES):
-            t = source_terms[24 * s : 24 * s + 24] * up
-            l = jnp.broadcast_to(source_terms[144 + s : 145 + s] * up, (16, ELEM))
+            t = values[24 * s : 24 * s + 24] * up
+            l = jnp.broadcast_to(values[144 + s : 145 + s] * up, (16, width))
             for p, part in enumerate(split8(jnp.concatenate([t, t], axis=0))):
-                t_parts[p, s] = part.astype(BF)
+                t_parts[p, s, :, e] = part.astype(BF)
             for p, part in enumerate(split8(l)):
-                l_parts[p, s] = part.astype(BF)
-        return down
-
-    terms_down = store_terms(rhs_terms)
+                l_parts[p, s, :, e] = part.astype(BF)
+
+    rhs_max = largest(rhs_terms[...])
+    gain = largest(row_sum)
+    terms_up, terms_down = factors(rhs_max)
+    for c in range(ELEM // CHUNK):
+        e = slice(c * CHUNK, (c + 1) * CHUNK)
+        store_terms(rhs_terms[:, e], e, terms_up)
 
     def row_ids(first, last, dtype):
         r = iota((16, ELEM), 0)
@@ -370,13 +373,19 @@
         step = scale[rows] * partial[rows]
         x = step if first else total[rows] + step
         total[rows] = x
-        up, down = scaling(x)
+        x_max = largest(x)
+        up, down = factors(x_max)
         for p, part in enumerate(split8(x * up)):
             table[p, rows] = part
-        return down
+        return down, x_max
 
     assemble("out", terms_down)
+    pl.semaphore_wait(barrier, 4)
     post(1, partial)
+    scale[...] = jnp.zeros_like(scale)
+    for a in range(OWN_BLOCKS, BLOCKS):
+        diag_block(a)
+    post(0, scale)
     for a in range(OWN_BLOCKS):
         diag_block(a)
     assemble("own", terms_down)
@@ -387,25 +396,35 @@
         scale[rows] = jnp.where(d == 0.0, 0.0, DAMPING / jnp.where(d == 0.0, 1.0, d))
 
     invert("own")
-    fetch("own", update("own", True))
+    for c in range(ELEM // CHUNK):
+        e = slice(c * CHUNK, (c + 1) * CHUNK)
+        potential[:, e] = pick(dot(left3[MATS * TP :], src3[:, e]), NP, e)[0:NODES]
+    for m in range(MATS):
+        hi, lo = split(dot3(split(inv_pad[m]), lift_t, dot_nt))
+        w3[NP * m : NP * (m + 1)] = jnp.concatenate([hi, hi, lo], axis=1)
+    down, own_max = update("own", True)
+    fetch("own", down)
     collect(0, scale)
     collect(1, partial)
     invert("out")
-    fetch("out", update("out", True))
+    down, out_max = update("out", True)
+    fetch("out", down)
 
     for sweep in range(SWEEPS - 1):
         gathered()
+        terms_up, terms_down = factors(rhs_max + gain * jnp.maximum(own_max, out_max))
         for c in range(ELEM // CHUNK):
             e = slice(c * CHUNK, (c + 1) * CHUNK)
             y = pick(dot(a3[...], x3[:, e]), TP, e)
-            terms[:, e] = rhs_terms[:, e] - y
-        terms_down = store_terms(terms)
+            store_terms(rhs_terms[:, e] - y, e, terms_up)
         assemble("out", terms_down)
         post(2 + sweep, partial)
         assemble("own", terms_down)
-        fetch("own", update("own", False))
+        down, own_max = update("own", False)
+        fetch("own", down)
         collect(2 + sweep, partial)
-        fetch("out", update("out", False))
+        down, out_max = update("out", False)
+        fetch("out", down)
 
     rows = slice(OWN_MAIN, OWN_LEFT + 16)
     back = jnp.zeros((304, 256), F32)
@@ -442,6 +461,15 @@
 
 
 def shards(source, inverses, lift, stab, material, face_slot, owner_map):
+    operands = (
+        source,
+        inverses.transpose(1, 0, 2),
+        lift.T,
+        stab.reshape(1, MATS),
+        material.reshape(1, ELEM),
+        face_slot,
+        owner_map,
+    )
     vmem = pl.BlockSpec(memory_space=pltpu.VMEM)
     hbm = pl.BlockSpec(memory_space=pltpu.HBM)
     v = pltpu.VMEM
@@ -475,7 +503,6 @@
             v((MATS * TP, 3 * TP), BF),
             v((MATS * NP, 3 * TP), BF),
             v((TP, ELEM), F32),
-            v((TP, ELEM), F32),
             v((SIDES, 24, ELEM), F32),
             v((SIDES, 8, ELEM), F32),
             v((3 * TP, ELEM), BF),
@@ -494,17 +521,9 @@
             pltpu.SemaphoreType.DMA((7,)),
         ],
         compiler_params=pltpu.CompilerParams(
-            collective_id=0, has_side_effects=True, vmem_limit_bytes=63 * 2**20
+            collective_id=0, has_side_effects=True, vmem_limit_bytes=48 * 2**20
         ),
-    )(
-        source,
-        inverses.transpose(1, 0, 2),
-        lift.T,
-        stab.reshape(1, MATS),
-        material.reshape(1, ELEM),
-        face_slot,
-        owner_map,
-    )
+    )(*(pltpu.with_memory_space_constraint(x, pltpu.HBM) for x in operands))
 
 
 def solution(mesh):

time: 43.7 us -> 38.9 us (0.89)
  Pallas kernels: 40.2 us -> 36.6 us
  local copies, waits for them, and re-layouts: 2.68 us -> 1.54 us
    pallas_call x1, Pallas kernels: 40.2 us -> 36.6 us  [shards(): pl.pallas_call(kernel, out_shape=(jax.ShapeDtypeStruct((NODES, ELEM), F32...]
    unnamed x4 -> x2, local copies, waits for them, and re-layouts: 2.68 us -> 1.54 us
where the time goes in v6:
time: 38.9 us; the launch traced here: 38.8 us
  Pallas kernels  36.6 us (94%)
  local copies, waits for them, and re-layouts  1.54 us (4%)
  between operations  0.64 us (2%)
    pallas_call x1, Pallas kernels, shards(): pl.pallas_call(kernel, out_shape=(jax.ShapeDtypeStruct((NODES, ELEM), F32...  36.6 us
    unnamed x2, local copies, waits for them, and re-layouts  1.54 us

profile of v6, /device:TPU:7, one launch (start us, length us, event | category | flops | bytes accessed | tf_op | source)
XLA Modules:
  0.0 38.8 jit_solution(3949613550286441315)
XLA Ops:
  0.6 36.6 %shard_map.86 = (f32[125,1024]{1,0:T(8,128)S(1)}, f32[25,3072]{1,0:T(8,128)S(1)}) custom-call(f32[125,1024]{1,0:T(8,128)} %source_hbm.1, f32[125,4,125]{2,1,0:T(4,128)} %bitcast.4, f32[150,125]{1,0:T(8,128)} %bitcast.5, f32[1,4]{1,0:T(1,128)} %bitcast.7, s32[1,1024]{1,0:T(1,128)} %bitcast.6, s32[6,1024]{1,0:T(8,128)} %face_slot_hbm.1, s32[1,768]{1,0:T(1,128)} %owner_map_hbm.1), custom_call_target="tpu_custom_call" | custom-call | tf_op jit(solution)/shard_map/pallas_call | solution.py:476
  37.3 0.8 %copy.11 = f32[125,1024]{1,0:T(8,128)} copy(f32[125,1024]{1,0:T(8,128)S(1)} %get-tuple-element.4) | data formatting | bytes 1024000
  38.1 0.7 %copy.12 = f32[25,3072]{1,0:T(8,128)} copy(f32[25,3072]{1,0:T(8,128)S(1)} %get-tuple-element.5) | data formatting | bytes 614400

commit v7 on v6

--- a/solution.py
+++ b/solution.py
@@ -305,13 +305,13 @@
 
     def store_terms(values, e, up):
         width = values.shape[1]
-        for s in range(SIDES):
-            t = values[24 * s : 24 * s + 24] * up
-            l = jnp.broadcast_to(values[144 + s : 145 + s] * up, (16, width))
-            for p, part in enumerate(split8(jnp.concatenate([t, t], axis=0))):
-                t_parts[p, s, :, e] = part.astype(BF)
-            for p, part in enumerate(split8(l)):
-                l_parts[p, s, :, e] = part.astype(BF)
+        for p, part in enumerate(split8(values * up)):
+            part = part.astype(F32)
+            for s in range(SIDES):
+                t = part[24 * s : 24 * s + 24]
+                t_parts[p, s, :, e] = jnp.concatenate([t, t], axis=0).astype(BF)
+                l = jnp.broadcast_to(part[144 + s : 145 + s], (16, width))
+                l_parts[p, s, :, e] = l.astype(BF)
 
     rhs_max = largest(rhs_terms[...])
     gain = largest(row_sum)

time: 38.9 us -> 38.6 us (level)
  no operation moved by 1% of the time
where the time goes in v7:
time: 38.6 us; the launch traced here: 38.5 us
  Pallas kernels  36.3 us (94%)
  local copies, waits for them, and re-layouts  1.54 us (4%)
  between operations  0.64 us (2%)
    pallas_call x1, Pallas kernels, shards(): pl.pallas_call(kernel, out_shape=(jax.ShapeDtypeStruct((NODES, ELEM), F32...  36.3 us
    unnamed x2, local copies, waits for them, and re-layouts  1.54 us

profile of v7, /device:TPU:7, one launch (start us, length us, event | category | flops | bytes accessed | tf_op | source)
XLA Modules:
  0.0 38.5 jit_solution(523254994196929298)
XLA Ops:
  0.6 36.3 %shard_map.86 = (f32[125,1024]{1,0:T(8,128)S(1)}, f32[25,3072]{1,0:T(8,128)S(1)}) custom-call(f32[125,1024]{1,0:T(8,128)} %source_hbm.1, f32[125,4,125]{2,1,0:T(4,128)} %bitcast.4, f32[150,125]{1,0:T(8,128)} %bitcast.5, f32[1,4]{1,0:T(1,128)} %bitcast.7, s32[1,1024]{1,0:T(1,128)} %bitcast.6, s32[6,1024]{1,0:T(8,128)} %face_slot_hbm.1, s32[1,768]{1,0:T(1,128)} %owner_map_hbm.1), custom_call_target="tpu_custom_call" | custom-call | tf_op jit(solution)/shard_map/pallas_call | solution.py:476
  36.9 0.8 %copy.11 = f32[125,1024]{1,0:T(8,128)} copy(f32[125,1024]{1,0:T(8,128)S(1)} %get-tuple-element.4) | data formatting | bytes 1024000
  37.7 0.7 %copy.12 = f32[25,3072]{1,0:T(8,128)} copy(f32[25,3072]{1,0:T(8,128)S(1)} %get-tuple-element.5) | data formatting | bytes 614400

commit v8 on v7

--- a/solution.py
+++ b/solution.py
@@ -298,7 +298,7 @@
             m_row == 0, y[0], jnp.where(m_row == 1, y[1], jnp.where(m_row == 2, y[2], y[3]))
         ).reshape(width, y.shape[3])
 
-    CHUNK = 512
+    CHUNK = 1024
     for c in range(ELEM // CHUNK):
         e = slice(c * CHUNK, (c + 1) * CHUNK)
         rhs_terms[:, e] = pick(dot(left3[0 : MATS * TP], src3[:, e]), TP, e)

time: 38.6 us -> 38.4 us (level)
  no operation moved by 1% of the time
where the time goes in v8:
time: 38.4 us; the launch traced here: 38.3 us
  Pallas kernels  36.1 us (94%)
  local copies, waits for them, and re-layouts  1.54 us (4%)
  between operations  0.64 us (2%)
    pallas_call x1, Pallas kernels, shards(): pl.pallas_call(kernel, out_shape=(jax.ShapeDtypeStruct((NODES, ELEM), F32...  36.1 us
    unnamed x2, local copies, waits for them, and re-layouts  1.54 us

profile of v8, /device:TPU:7, one launch (start us, length us, event | category | flops | bytes accessed | tf_op | source)
XLA Modules:
  0.0 38.3 jit_solution(4569847007061646468)
XLA Ops:
  0.6 36.1 %shard_map.86 = (f32[125,1024]{1,0:T(8,128)S(1)}, f32[25,3072]{1,0:T(8,128)S(1)}) custom-call(f32[125,1024]{1,0:T(8,128)} %source_hbm.1, f32[125,4,125]{2,1,0:T(4,128)} %bitcast.4, f32[150,125]{1,0:T(8,128)} %bitcast.5, f32[1,4]{1,0:T(1,128)} %bitcast.7, s32[1,1024]{1,0:T(1,128)} %bitcast.6, s32[6,1024]{1,0:T(8,128)} %face_slot_hbm.1, s32[1,768]{1,0:T(1,128)} %owner_map_hbm.1), custom_call_target="tpu_custom_call" | custom-call | tf_op jit(solution)/shard_map/pallas_call | solution.py:476
  36.8 0.8 %copy.11 = f32[125,1024]{1,0:T(8,128)} copy(f32[125,1024]{1,0:T(8,128)S(1)} %get-tuple-element.4) | data formatting | bytes 1024000
  37.6 0.7 %copy.12 = f32[25,3072]{1,0:T(8,128)} copy(f32[25,3072]{1,0:T(8,128)S(1)} %get-tuple-element.5) | data formatting | bytes 614400
